TPU v7x, 256 devices: a whole 4x4x8 slice. The times are simulated.
256 devices in a mesh: section: 32 (over z, x_lo, core), tp: 8 (over y, x_hi).
Axes of the slice: x: 4 (x_hi: 2, x_lo: 2; x = x_hi * 2 + x_lo), y: 4, z: 8, core: 2. Of those that a mesh axis runs over, the one named last changes fastest.
Arguments:
- layer_outputs: bfloat16 [32, 128, 8192], P('section', None, 'tp'), may hold values from -72 to 72
- stream_grads: bfloat16 [32, 3, 128, 8192], P('section', None, None, 'tp'), may hold values from -0.3125 to 0.3125
- residual_grads: bfloat16 [32, 128, 8192], P('section', None, 'tp'), may hold values from -0.4375 to 0.4375
- norm_gain: bfloat16 [32, 8192], P('section', 'tp'), may hold values from 0.5 to 1.5
- first_weight: bfloat16 [32, 8192, 384], P('section', 'tp'), may hold values from -0.0625 to 0.0625
- second_weight: bfloat16 [32, 384, 96], P('section'), may hold values from -0.3125 to 0.3125
Outputs:
- stream_grad: bfloat16 [32, 128, 8192], P('section', None, 'tp')
- first_grad: float32 [32, 8192, 384], P('section', 'tp')
- second_grad: float32 [32, 384, 96], P('section')
All inputs are finite; a program needn't handle non-finite values.
Results may differ from a plain program's by a relative error of at most 0.008.
Values may be sent and summed in bfloat16 or wider, within the bound.
A program may use at most 128 MiB of HBM per device.

v0:
```python
import jax
import jax.numpy as jnp
from jax import lax
from jax.sharding import PartitionSpec as P


def entering(x, axis, combine, identity):
    devices, here = (lax.axis_size(axis), lax.axis_index(axis))
    everything = lax.all_gather(x.astype(jnp.bfloat16), axis)
    start = jnp.broadcast_to(jnp.asarray(identity, x.dtype), x.shape)

    def hop(k, before):
        at = devices - 1 - k
        reached = at > here
        new = combine(before, everything[at].astype(x.dtype))
        return jnp.where(reached, new, before)

    return lax.fori_loop(0, devices, hop, start)


def gelu_grad(pre_act, upstream):
    value, pullback = jax.vjp(jax.nn.gelu, pre_act)
    return pullback(upstream)[0]


def add_terms(earlier, later_term):
    return earlier + later_term


def local(layer_outputs, stream_grads, residual_grads, norm_gain, first_weight, second_weight):
    position = lax.axis_index("section")
    depth = lax.axis_size("section")
    inputs = layer_outputs[0].astype(jnp.float32)
    tokens = inputs.shape[0]
    full_width = inputs.shape[1] * lax.axis_size("tp")
    squares = lax.psum(jnp.sum(inputs * inputs, axis=1), "tp")
    inverse = lax.rsqrt(squares / full_width + 1e-05)[:, None]
    gain_row = norm_gain[0].astype(jnp.float32)
    normed = (inputs * inverse * gain_row).astype(jnp.bfloat16)
    pre_part = jnp.dot(normed, first_weight[0], preferred_element_type=jnp.float32)
    pre_act = lax.psum(pre_part, "tp")
    hidden = jax.nn.gelu(pre_act)
    second = second_weight[0].astype(jnp.float32)
    depth_mask = jnp.arange(depth, dtype=jnp.int32) <= position
    mixing = jnp.dot(hidden, second, precision=lax.Precision.HIGHEST).reshape(tokens, 3, depth)
    mixing = jnp.where(depth_mask[None, None, :], mixing, 0.0)
    mixing_low = mixing.astype(jnp.bfloat16)
    streams = stream_grads[0]
    resid_own = residual_grads[0].astype(jnp.float32)
    contrib = jnp.einsum(
        "std,jtd->tsj",
        streams,
        lax.all_gather(layer_outputs, "section", axis=0, tiled=True),
        preferred_element_type=jnp.float32,
    )
    local_terms = contrib
    local_terms = jnp.where(depth_mask[None, None, :], local_terms, 0.0)
    mix_grad = lax.psum(local_terms, "tp")
    block = jnp.einsum("tsj,std->jtd", mixing_low, streams, preferred_element_type=jnp.float32)
    summed = lax.psum_scatter(block, "section", scatter_dimension=0, tiled=True)
    flat_grad = mix_grad.reshape(tokens, 3 * depth)
    second_grad = jnp.dot(hidden.T, flat_grad, precision=lax.Precision.HIGHEST)
    hidden_grad = jnp.dot(flat_grad, second.T, precision=lax.Precision.HIGHEST)
    pre_grad = gelu_grad(pre_act, hidden_grad).astype(jnp.bfloat16)
    first_grad = jnp.dot(normed.T, pre_grad, preferred_element_type=jnp.float32)
    normed_grad = jnp.dot(pre_grad, first_weight[0].T, preferred_element_type=jnp.float32)
    scaled = normed_grad * gain_row
    along = lax.psum(jnp.sum(scaled * inputs, axis=1), "tp")
    local_grad = inverse * scaled - inputs * inverse**3 * along[:, None] / full_width
    zeros_like_own = jnp.zeros_like(resid_own)
    later_sum = entering(resid_own, "section", add_terms, zeros_like_own)
    carried = later_sum + resid_own
    total = summed[0] + carried + local_grad
    return (total.astype(jnp.bfloat16)[None], first_grad[None], second_grad[None])


def solution(mesh):
    placed = (
        P("section", None, "tp"),
        P("section", None, None, "tp"),
        P("section", None, "tp"),
        P("section", "tp"),
        P("section", "tp", None),
        P("section", None, None),
    )
    return jax.shard_map(
        local,
        mesh=mesh,
        in_specs=placed,
        out_specs=(P("section", None, "tp"), P("section", "tp", None), P("section", None, None)),
        check_vma=False,
    )
```

profile of v0, /device:TPU:1, one launch (start us, length us, event | category | flops | bytes accessed | tf_op | source)
XLA Modules:
  0.0 495.1 jit_solution(13607809840191176451)
XLA Ops:
  9.8 76.7 %all-gather.5.cloned.1.call-done = bf16[32,128,1024]{2,1,0:T(8,128)(2,1)} async-done(((bf16[1,128,1024]{2,1,0:T(8,128)(2,1)}), bf16[32,128,1024]{2,1,0:T(8,128)(2,1)}) %all-gather.5.cloned.1.call-update) | async-done | bytes 8388624 | tf_op jit(solution)/shard_map/all_gather | solution.py:53
  86.4 8.5 %fusion = f32[128,3,32]{2,1,0:T(4,128)S(1)} fusion(bf16[32,128,1024]{2,1,0:T(8,128)(2,1)} %all-gather.5.cloned.1.call-done, bf16[3,128,1024]{2,1,0:T(8,128)(2,1)} %bitcast.80), kind=kOutput, calls=%fused_computation.2 | convolution fusion | flops 25165824 | bytes 9224192 | tf_op jit(solution)/shard_map/std,jtd->tsj/dot_general | solution.py:50
  95.1 35.2 %all-reduce = (f32[128]{0:T(128)S(1)}, f32[128,96]{0,1:T(8,128)S(1)}) all-reduce(f32[128]{0:T(128)S(1)} %fusion.12, f32[128,96]{0,1:T(8,128)S(1)} %bitcast.82), channel_id=1, replica_groups=mesh['section'=32,'tp'=8] {'tp'}, use_global_device_ids=true, to_apply=%region_1.0 | all-reduce | flops 12416 | bytes 99328 | tf_op jit(solution)/shard_map/psum | solution.py:36
  132.5 84.9 %all-reduce.3.cloned.1.call-done = f32[128,384]{1,0:T(8,128)} async-done(((f32[128,384]{1,0:T(8,128)}), f32[128,384]{1,0:T(8,128)}) %all-reduce.3.cloned.1.call-update) | async-done | bytes 196624 | tf_op jit(solution)/shard_map/psum | solution.py:41
  217.4 1.2 fusion.2
  218.8 2.4 convolution_bitcast_fusion
  221.2 19.0 %copy.18 = f32[32,128,1024]{2,1,0:T(8,128)} copy(f32[32,128,1024]{2,0,1:T(8,128)S(1)} %convolution_bitcast_fusion) | data formatting | bytes 33554432 | tf_op jit(solution)/shard_map/tsj,std->jtd/transpose | solution.py:59
  240.2 54.9 %all-gather.3.cloned.1.call-done = bf16[32,128,1024]{2,1,0:T(8,128)(2,1)} async-done(((bf16[1,128,1024]{2,1,0:T(8,128)(2,1)}), bf16[32,128,1024]{2,1,0:T(8,128)(2,1)}) %all-gather.3.cloned.1.call-update) | async-done | bytes 8388624 | tf_op jit(solution)/shard_map/all_gather | solution.py:9
  295.1 40.5 %while.16 = (s32[]{:T(128)}, f32[128,1024]{1,0:T(8,128)S(1)}, s32[]{:T(128)}, bf16[32,128,1024]{2,1,0:T(8,128)(2,1)}, s32[]{:T(128)}, /*index=5*/s32[]{:T(128)}, s32[]{:T(128)}, s32[]{:T(128)}) while((s32[]{:T(128)}, f32[128,1024]{1,0:T(8,128)S(1)}, s32[]{:T(128)}, bf16[32,128,1024]{2,1,0:T(8,128)(2,1)}, s32[]{:T(128)}, ...), condition=%wide.region_5.6_spmd.clone, body=%wide.region_4.5_spmd.clone.sunk | while | flops 524296 | bytes 1310875 | solution.py:18
  307.8 1.3 add_select_fusion.2
  309.0 1.2 add_select_fusion.2
  312.8 1.2 add_select_fusion.2
  314.1 1.2 add_select_fusion.2
  320.4 1.2 add_select_fusion.2
  325.5 1.2 add_select_fusion.2
  326.8 1.2 add_select_fusion.2
  328.0 1.2 add_select_fusion.2
  329.3 1.2 add_select_fusion.2
  331.8 1.2 add_select_fusion.2
  333.1 1.2 add_select_fusion.2
  336.5 22.3 %psum.31 = f32[128]{0:T(128)S(1)} all-reduce(f32[128]{0:T(128)S(1)} %get-tuple-element.141), channel_id=1, replica_groups=mesh['section'=32,'tp'=8] {'tp'}, use_global_device_ids=true, to_apply=%region_8.9 | all-reduce | flops 128 | bytes 1024 | tf_op jit(solution)/shard_map/psum | solution.py:68
  359.8 1.6 convolution_bitcast_fusion.1
  361.4 125.1 %reduce-scatter.2.cloned.1.call-done = f32[1,128,1024]{2,1,0:T(8,128)} async-done(((f32[32,128,1024]{2,1,0:T(8,128)}), f32[1,128,1024]{2,1,0:T(8,128)}) %reduce-scatter.2.cloned.1.call-update) | async-done | bytes 524304 | tf_op jit(solution)/shard_map/reduce_scatter | solution.py:60
  486.5 2.1 fusion.27
  (53 shorter events, 32.7 us)
Async XLA Ops:
  7.2 123.3 %copy-start = (bf16[1,1024,384]{2,1,0:T(8,128)(2,1)S(1)}, bf16[1,1024,384]{2,1,0:T(8,128)(2,1)}, u32[]{:S(2)}) copy-start(bf16[1,1024,384]{2,1,0:T(8,128)(2,1)} %param.12) | copy-start | bytes 2359300
  7.2 123.2 %copy-start.1 = (bf16[1,128,1024]{2,1,0:T(8,128)(2,1)S(1)}, bf16[1,128,1024]{2,1,0:T(8,128)(2,1)}, u32[]{:S(2)}) copy-start(bf16[1,128,1024]{2,1,0:T(8,128)(2,1)} %param.8) | copy-start | bytes 786436
  7.2 211.6 %copy-start.2 = (bf16[1,3,128,1024]{3,2,1,0:T(8,128)(2,1)S(1)}, bf16[1,3,128,1024]{3,2,1,0:T(8,128)(2,1)}, u32[]{:S(2)}) copy-start(bf16[1,3,128,1024]{3,2,1,0:T(8,128)(2,1)} %param.9) | copy-start | bytes 2359300
  7.2 210.2 %copy-start.5 = (bf16[1,384,96]{1,2,0:T(8,128)(2,1)S(1)}, bf16[1,384,96]{1,2,0:T(8,128)(2,1)}, u32[]{:S(2)}) copy-start(bf16[1,384,96]{1,2,0:T(8,128)(2,1)} %param.13) | copy-start | bytes 221188
  7.2 79.2 %all-gather.5.cloned.1.call-start = ((), (), s32[]{:S(2)}) async-start(), calls=%async_computation.4 | async-start | bytes 8650752 | tf_op jit(solution)/shard_map/all_gather | solution.py:53
  7.9 209.4 %all-reduce.3.cloned.1.call-start = ((), (), s32[]{:S(2)}) async-start(), calls=%async_computation.1 | async-start | bytes 393216 | tf_op jit(solution)/shard_map/psum | solution.py:41
  131.5 163.6 %all-gather.3.cloned.1.call-start = ((), (), s32[]{:S(2)}) async-start(), calls=%async_computation.3 | async-start | bytes 8650752 | tf_op jit(solution)/shard_map/all_gather | solution.py:9
  132.2 354.3 %reduce-scatter.2.cloned.1.call-start = ((), (), s32[]{:S(2)}) async-start(), calls=%async_computation.2 | async-start | bytes 17301504 | tf_op jit(solution)/shard_map/reduce_scatter | solution.py:60
  240.2 95.5 %copy-start.4 = (f32[128,384]{1,0:T(8,128)S(1)}, f32[128,384]{1,0:T(8,128)}, u32[]{:S(2)}) copy-start(f32[128,384]{1,0:T(8,128)} %all-reduce.3.cloned.1.call-done) | copy-start | bytes 589828
  240.2 246.3 %copy-start.3 = (bf16[1,128,1024]{2,1,0:T(8,128)(2,1)S(1)}, bf16[1,128,1024]{2,1,0:T(8,128)(2,1)}, u32[]{:S(2)}) copy-start(bf16[1,128,1024]{2,1,0:T(8,128)(2,1)} %param.10) | copy-start | bytes 786436
Sparse Core Ops, SparseCore 0:
  9.9 76.4 all-gather.4
  131.6 85.7 all-reduce.2
  219.4 75.6 all-gather.2
  297.7 188.7 reduce-scatter.1
where the time goes:
time: 496 us; the launch traced here: 495 us
  waiting for transfers between devices  343 us (69%)
  blocking collectives  57.5 us (12%)
  other arithmetic  43.5 us (9%)
  local copies, waits for them, and re-layouts  19.3 us (4%)
  matrix products  16.6 us (3%)
  between operations  13.9 us (3%)
    reduce_scatter x1, waiting for transfers between devices, local(): summed = lax.psum_scatter(block, 'section', scatter_dimension=0, tiled=True)  125 us
    psum x1, waiting for transfers between devices, local(): pre_act = lax.psum(pre_part, 'tp')  84.9 us
    all_gather x1, waiting for transfers between devices, local(): lax.all_gather(layer_outputs, 'section', axis=0, tiled=True)  76.7 us
    all_gather x1, waiting for transfers between devices, entering(): everything = lax.all_gather(x.astype(jnp.bfloat16), axis)  54.9 us
    select_n x32, other arithmetic, hop(): return jnp.where(reached, new, before)  39.6 us
    psum x1, blocking collectives, local(): squares = lax.psum(jnp.sum(inputs * inputs, axis=1), 'tp')  35.2 us
    psum x1, blocking collectives, local(): along = lax.psum(jnp.sum(scaled * inputs, axis=1), 'tp')  22.3 us
    transpose x1, local copies, waits for them, and re-layouts, local(): jnp.einsum('tsj,std->jtd', mixing_low, streams, preferred_element_type=jn...  19 us
  transfers between devices with their start and end apart: 4, of which 4 were waited for; matrix products, arithmetic and copies ran while one was open for 14% of the time, Pallas kernels for 0%

commit v1 on v0

v1 whole, which is shorter than its diff:
```python
import functools

import jax
import jax.numpy as jnp
from jax import lax
from jax.experimental import pallas as pl
from jax.experimental.pallas import tpu as pltpu
from jax.sharding import PartitionSpec as P

MESH = pl.DeviceIdType.MESH
F32, BF16 = jnp.float32, jnp.bfloat16
SECTIONS, SHARDS = 32, 8
TOKENS, WIDTH, HIDDEN = 128, 1024, 384
FULL_WIDTH = WIDTH * SHARDS
C0, C1 = 0.7978845608028654, 0.044715


def dot(a, b):
    return jnp.dot(a, b, preferred_element_type=F32)


def dot_nt(a, b):
    return lax.dot_general(a, b, (((1,), (1,)), ((), ())), preferred_element_type=F32)


def dot_tn(a, b):
    return lax.dot_general(a, b, (((0,), (0,)), ((), ())), preferred_element_type=F32)


def halves(v):
    high = v.astype(BF16)
    return high, (v - high.astype(F32)).astype(BF16)


def grid(rows, columns):
    return (
        lax.broadcasted_iota(jnp.int32, (rows, columns), 0),
        lax.broadcasted_iota(jnp.int32, (rows, columns), 1),
    )


def pick(condition):
    return jnp.where(condition, 1.0, 0.0).astype(BF16)


def kernel(
    x_hbm, g_hbm, r_hbm, gain_ref, w1_hbm, w2_ref,
    out_hbm, first_hbm, second_hbm,
    stage, r_stage, w1, sent, held, r_sent, r_held, w_sent, w_held, o_sent, o_held,
    z_sent, z_held, act, d_sent, d_held, e_sent, e_held,
    out_v, first_v, second_v, normed_t,
    in_sem, out_sem, x_ss, x_rs, r_ss, r_rs, w_ss, w_rs, o_ss, o_rs,
    z_ss, z_rs, a_ss, a_rs, d_ss, d_rs, e_ss, e_rs,
):
    me = lax.axis_index("section")
    part = lax.axis_index("tp")

    loads = []
    for b in range(2):
        rows = pl.ds(64 * b, 64)
        for s in range(3):
            loads.append(pltpu.make_async_copy(g_hbm.at[0, s, rows], stage.at[b, s], in_sem.at[len(loads)]))
        loads.append(pltpu.make_async_copy(x_hbm.at[0, rows], stage.at[b, 3], in_sem.at[len(loads)]))
    loads.append(pltpu.make_async_copy(w1_hbm.at[0], w1, in_sem.at[len(loads)]))
    for b in range(2):
        for f in range(4):
            loads.append(
                pltpu.make_async_copy(
                    r_hbm.at[0, pl.ds(64 * b, 64), pl.ds(256 * f, 256)], r_stage.at[b, f], in_sem.at[len(loads)]
                )
            )
    for load in loads:
        load.start()

    barrier = pltpu.get_barrier_semaphore()

    def greet_section(n, c):
        pl.semaphore_signal(barrier, inc=1, device_id={"section": lax.rem(me + n, SECTIONS)}, device_id_type=MESH)
        return c

    def greet_part(n, c):
        pl.semaphore_signal(barrier, inc=1, device_id={"tp": lax.rem(part + n, SHARDS)}, device_id_type=MESH)
        return c

    lax.fori_loop(1, SECTIONS, greet_section, 0)
    lax.fori_loop(1, SHARDS, greet_part, 0)

    def section_copy(src, dst, ss, rs, to, slot):
        return pltpu.make_async_remote_copy(
            src_ref=src.at[to], dst_ref=dst.at[slot], send_sem=ss.at[to], recv_sem=rs.at[slot],
            device_id={"section": to}, device_id_type=MESH,
        )

    def part_copy(src, dst, ss, rs, to, slot):
        return pltpu.make_async_remote_copy(
            src_ref=src, dst_ref=dst.at[slot], send_sem=ss.at[to], recv_sem=rs.at[slot],
            device_id={"tp": to}, device_id_type=MESH,
        )

    def send_sections(src, dst, ss, rs):
        def step(n, c):
            section_copy(src, dst, ss, rs, lax.rem(me + n, SECTIONS), me).start()
            return c

        lax.fori_loop(1, SECTIONS, step, 0)

    def await_sections(src, dst, ss, rs):
        def step(n, c):
            peer = lax.rem(me + n, SECTIONS)
            section_copy(src, dst, ss, rs, peer, peer).wait_recv()
            return c

        lax.fori_loop(1, SECTIONS, step, 0)

    def drain_sections(src, dst, ss, rs):
        def step(n, c):
            section_copy(src, dst, ss, rs, lax.rem(me + n, SECTIONS), me).wait_send()
            return c

        lax.fori_loop(1, SECTIONS, step, 0)

    def send_parts(pick_src, dst, ss, rs):
        def step(n, c):
            peer = lax.rem(part + n, SHARDS)
            part_copy(pick_src(peer), dst, ss, rs, peer, part).start()
            return c

        lax.fori_loop(1, SHARDS, step, 0)

    def await_parts(pick_src, dst, ss, rs):
        def step(n, c):
            peer = lax.rem(part + n, SHARDS)
            part_copy(pick_src(peer), dst, ss, rs, peer, peer).wait_recv()
            return c

        lax.fori_loop(1, SHARDS, step, 0)

    def drain_parts(pick_src, dst, ss, rs):
        def step(n, c):
            peer = lax.rem(part + n, SHARDS)
            part_copy(pick_src(peer), dst, ss, rs, peer, part).wait_send()
            return c

        lax.fori_loop(1, SHARDS, step, 0)

    row, col = grid(256, 256)
    regroup = pick(((row >> 2) & 3) * 64 + (row >> 4) * 4 + (row & 3) == col)

    gain = gain_ref[...].astype(F32)

    for b in range(2):
        for load in loads[4 * b : 4 * b + 4]:
            load.wait()
        grouped = dot(regroup, stage[b].reshape(256, WIDTH)).astype(BF16)
        sent[pl.ds(16 * b, 16)] = grouped.reshape(16, 16, WIDTH)

    loads[8].wait()
    for b in range(2):
        x = stage[b, 3].astype(F32)
        high, low = halves(x * gain)
        product = dot(high, w1[...]) + dot(low, w1[...])
        squares = jnp.sum(x * x, axis=1, keepdims=True)
        block = jnp.concatenate([product, jnp.broadcast_to(squares, (64, 128))], axis=1)
        z_sent[pl.ds(4 * b, 4)] = block.reshape(4, 16, 512)

    pl.semaphore_wait(barrier, SECTIONS - 1 + SHARDS - 1)

    z_src = lambda peer: z_sent.at[peer]
    send_parts(z_src, z_held, z_ss, z_rs)
    send_sections(sent, held, x_ss, x_rs)
    held[pl.ds(me, 1)] = sent[pl.ds(me, 1)]
    z_held[pl.ds(part, 1)] = z_sent[pl.ds(part, 1)]

    for load in loads[9:]:
        load.wait()
    for b in range(2):
        grouped = dot(regroup, r_stage[b].reshape(256, 256)).astype(BF16)
        r_sent[pl.ds(16 * b, 16)] = grouped.reshape(16, 16, 256)
    r_held[pl.ds(me, 1)] = r_sent[pl.ds(me, 1)]

    await_parts(z_src, z_held, z_ss, z_rs)
    total = z_held[0]
    for p in range(1, SHARDS):
        total = total + z_held[p]
    scale = lax.rsqrt(total[:, HIDDEN:] / FULL_WIDTH + 1e-05)
    own = jnp.concatenate([total[:, :HIDDEN] * scale[:, :1], scale], axis=1)
    act[pl.ds(part, 1)] = own.reshape(1, 16, 512)
    a_src = lambda peer: act.at[part]
    send_parts(a_src, act, a_ss, a_rs)
    send_sections(r_sent, r_held, r_ss, r_rs)
    row, col = grid(96, HIDDEN)
    w2 = w2_ref[0]
    w2_wide = dot(w2, pick(row == col >> 2)).astype(BF16)
    row, col = grid(96, 128)
    w2_pad = dot(w2, pick(row == col)).astype(BF16)
    await_parts(a_src, act, a_ss, a_rs)

    pre = act[:, :, :HIDDEN].reshape(TOKENS, HIDDEN)
    inverse = act[:, :, HIDDEN:].reshape(TOKENS, 128)[:, :1]
    square = pre * pre
    bend = jnp.tanh(C0 * pre * (1.0 + C1 * square))
    hidden = 0.5 * pre * (1.0 + bend)
    slope = 0.5 * (1.0 + bend) + 0.5 * pre * (1.0 - bend * bend) * (C0 * (1.0 + 3.0 * C1 * square))
    h_high, h_low = halves(hidden)
    mixing = dot(h_high, w2_wide) + dot(h_low, w2_wide)
    row, col = grid(TOKENS, HIDDEN)
    keep = ((row & 3) == (col & 3)) & (((col >> 2) & 31) <= me)
    mixing = jnp.where(keep, mixing, 0.0).astype(BF16)
    for b in range(2):
        block = mixing[64 * b : 64 * b + 64]
        stacked = jnp.concatenate(
            [block[:, :128], block[:, 128:256], block[:, 256:], jnp.zeros((64, 128), BF16)], axis=0
        )
        w_sent[pl.ds(16 * b, 16)] = dot(regroup, stacked).astype(BF16).reshape(16, 16, 128)
    w_held[pl.ds(me, 1)] = w_sent[pl.ds(me, 1)]
    send_sections(w_sent, w_held, w_ss, w_rs)

    for b in range(2):
        x = stage[b, 3].astype(F32)
        normed = (x * inverse[64 * b : 64 * b + 64] * gain).astype(BF16)
        normed_t[:, pl.ds(64 * b, 64)] = normed.T

    await_sections(sent, held, x_ss, x_rs)
    table = held[...].reshape(512, WIDTH)
    row, col = grid(128, 512)
    streams = dot(pick((row >> 2) * 16 + 12 + (row & 3) == col), table).astype(BF16)
    gram = dot_nt(table, streams)
    row, col = grid(512, 128)
    gram = jnp.where((row & 3) == (col & 3), gram, 0.0)
    rr, cc = grid(128, 128)
    spread = pick((rr >> 2) == (cc & 31))
    high, low = halves(gram)
    wide = dot(high, spread) + dot(low, spread)
    which = (row >> 2) & 3
    wide = jnp.where((which == (col >> 5)) & (which < 3) & ((col & 31) <= (row >> 4)), wide, 0.0)
    row, col = grid(128, 512)
    fold = pick(((row >> 2) == (col >> 4)) & ((row & 3) == (col & 3)))
    high, low = halves(wide)
    d_sent[...] = (dot(fold, high) + dot(fold, low)).reshape(SHARDS, 16, 128)
    d_src = lambda peer: d_sent.at[peer]
    send_parts(d_src, d_held, d_ss, d_rs)
    d_held[pl.ds(part, 1)] = d_sent[pl.ds(part, 1)]

    await_sections(w_sent, w_held, w_ss, w_rs)
    weights = w_held[...].reshape(512, 128).T
    partial = [dot(weights, table[:, 256 * f : 256 * f + 256]) for f in range(4)]
    await_sections(r_sent, r_held, r_ss, r_rs)
    row, col = grid(512, 512)
    later = pick(((row & 15) == (col & 15)) & ((col >> 4) >= (row >> 4)))
    carried = dot(later, r_held[...].reshape(512, 256))
    for b in range(2):
        stacked = jnp.concatenate([p[64 * b : 64 * b + 64] for p in partial], axis=0)
        high, low = halves(stacked)
        block = dot(regroup, high) + dot(regroup, low) + carried[256 * b : 256 * b + 256]
        o_sent[pl.ds(16 * b, 16)] = block.astype(BF16).reshape(16, 16, 256)
    o_held[pl.ds(me, 1)] = o_sent[pl.ds(me, 1)]

    await_parts(d_src, d_held, d_ss, d_rs)
    total = d_held[0]
    for p in range(1, SHARDS):
        total = total + d_held[p]
    for a in range(4):
        e_sent[a] = total[4 * a : 4 * a + 4]

    def e_copy(n):
        a, b = n // SHARDS, lax.rem(n, SHARDS)
        to = 4 * part + a
        return (to != me) | (b != part), pltpu.make_async_remote_copy(
            src_ref=e_sent.at[a], dst_ref=e_held.at[me], send_sem=e_ss.at[n], recv_sem=e_rs.at[me],
            device_id={"section": to, "tp": b}, device_id_type=MESH,
        )

    def e_send(n, c):
        away, copy = e_copy(n)

        @pl.when(away)
        def _():
            copy.start()

        return c

    def e_drain(n, c):
        away, copy = e_copy(n)

        @pl.when(away)
        def _():
            copy.wait_send()

        return c

    def e_await(n, c):
        @pl.when((n != me) | (me // 4 != part))
        def _():
            pltpu.make_async_remote_copy(
                src_ref=e_sent.at[0], dst_ref=e_held.at[n], send_sem=e_ss.at[0], recv_sem=e_rs.at[n],
                device_id={"section": n, "tp": me // 4}, device_id_type=MESH,
            ).wait_recv()

        return c

    lax.fori_loop(0, 32, e_send, 0)

    @pl.when(me // 4 == part)
    def _():
        e_held[pl.ds(me, 1)] = e_sent[pl.ds(lax.rem(me, 4), 1)]

    send_sections(o_sent, o_held, o_ss, o_rs)
    lax.fori_loop(0, SECTIONS, e_await, 0)

    mix_grad = e_held[...].reshape(TOKENS, 128)
    g_high, g_low = halves(mix_grad)
    pre_grad = ((dot_nt(g_high, w2_pad) + dot_nt(g_low, w2_pad)) * slope).astype(BF16)
    first_v[...] = dot(normed_t[...], pre_grad)
    first_out = pltpu.make_async_copy(first_v, first_hbm.at[0], out_sem.at[0])
    first_out.start()
    second = dot_tn(h_high, g_high) + dot_tn(h_high, g_low) + dot_tn(h_low, g_high)
    second_v[...] = second[:, :96]
    second_out = pltpu.make_async_copy(second_v, second_hbm.at[0], out_sem.at[1])
    second_out.start()
    along = jnp.sum(pre_grad.astype(F32) * pre, axis=1, keepdims=True)
    inner = inverse * inverse * along / FULL_WIDTH
    local = inverse * (dot_nt(pre_grad, w1[...]) * gain)

    await_sections(o_sent, o_held, o_ss, o_rs)
    for b in range(2):
        rows = slice(64 * b, 64 * b + 64)
        arrived = dot_tn(regroup, o_held[pl.ds(16 * b, 16)].reshape(256, 256))
        x = stage[b, 3].astype(F32)
        for f in range(4):
            lanes = slice(256 * f, 256 * f + 256)
            value = arrived[64 * f : 64 * f + 64] + (local[rows, lanes] - x[:, lanes] * inner[rows])
            out_v[pl.ds(64 * b, 64), pl.ds(256 * f, 256)] = value.astype(BF16)
    out_copy = pltpu.make_async_copy(out_v, out_hbm.at[0], out_sem.at[2])
    out_copy.start()

    drain_parts(z_src, z_held, z_ss, z_rs)
    drain_parts(a_src, act, a_ss, a_rs)
    drain_parts(d_src, d_held, d_ss, d_rs)
    drain_sections(sent, held, x_ss, x_rs)
    drain_sections(r_sent, r_held, r_ss, r_rs)
    drain_sections(w_sent, w_held, w_ss, w_rs)
    drain_sections(o_sent, o_held, o_ss, o_rs)
    lax.fori_loop(0, 32, e_drain, 0)
    first_out.wait()
    second_out.wait()
    out_copy.wait()


def local(layer_outputs, stream_grads, residual_grads, norm_gain, first_weight, second_weight):
    anywhere = pl.BlockSpec(memory_space=pl.ANY)
    vmem = pl.BlockSpec(memory_space=pltpu.VMEM)
    dma = pltpu.SemaphoreType.DMA
    by_section = lambda rows, lanes, dtype: pltpu.VMEM((SECTIONS, rows, lanes), dtype)
    by_part = lambda rows, lanes: pltpu.VMEM((SHARDS, rows, lanes), F32)
    return pl.pallas_call(
        kernel,
        out_shape=(
            jax.ShapeDtypeStruct((1, TOKENS, WIDTH), BF16),
            jax.ShapeDtypeStruct((1, WIDTH, HIDDEN), F32),
            jax.ShapeDtypeStruct((1, HIDDEN, 96), F32),
        ),
        in_specs=[anywhere, anywhere, anywhere, vmem, anywhere, vmem],
        out_specs=(anywhere, anywhere, anywhere),
        scratch_shapes=[
            pltpu.VMEM((2, 4, 64, WIDTH), BF16),
            pltpu.VMEM((2, 4, 64, 256), BF16),
            pltpu.VMEM((WIDTH, HIDDEN), BF16),
            by_section(16, WIDTH, BF16), by_section(16, WIDTH, BF16),
            by_section(16, 256, BF16), by_section(16, 256, BF16),
            by_section(16, 128, BF16), by_section(16, 128, BF16),
            by_section(16, 256, BF16), by_section(16, 256, BF16),
            by_part(16, 512), by_part(16, 512), by_part(16, 512),
            by_part(16, 128), by_part(16, 128),
            pltpu.VMEM((4, 4, 128), F32),
            by_section(4, 128, F32),
            pltpu.VMEM((TOKENS, WIDTH), BF16),
            pltpu.VMEM((WIDTH, HIDDEN), F32),
            pltpu.VMEM((HIDDEN, 96), F32),
            pltpu.VMEM((WIDTH, TOKENS), BF16),
            dma((17,)), dma((3,)),
            *[dma((SECTIONS,)) for _ in range(8)],
            *[dma((SHARDS,)) for _ in range(6)],
            dma((32,)), dma((32,)),
        ],
        compiler_params=pltpu.CompilerParams(
            collective_id=0, has_side_effects=True, vmem_limit_bytes=40 * 1024 * 1024
        ),
    )(layer_outputs, stream_grads, residual_grads, norm_gain, first_weight, second_weight)


def solution(mesh):
    placed = (
        P("section", None, "tp"),
        P("section", None, None, "tp"),
        P("section", None, "tp"),
        P("section", "tp"),
        P("section", "tp", None),
        P("section", None, None),
    )
    return jax.shard_map(
        local,
        mesh=mesh,
        in_specs=placed,
        out_specs=(P("section", None, "tp"), P("section", "tp", None), P("section", None, None)),
        check_vma=False,
    )
```

time: 496 us -> 75.9 us (0.15)
  waiting for transfers between devices: 343 us -> 0 us
  Pallas kernels: 0 us -> 65.5 us
  blocking collectives: 57.5 us -> 0 us
  other arithmetic: 43.5 us -> 0 us
  matrix products: 16.6 us -> 0 us
  between operations: 13.9 us -> 0.66 us
  local copies, waits for them, and re-layouts: 19.3 us -> 8.48 us
    all_gather x2 -> x0, waiting for transfers between devices: 132 us -> none  [the longest x1 76.7 us: local(): lax.all_gather(layer_outputs, 'section', axis=0, tiled=True)]
    reduce_scatter x1 -> x0, waiting for transfers between devices: 125 us -> none  [local(): summed = lax.psum_scatter(block, 'section', scatter_dimension=0, tiled=True)]
    psum x1 -> x0, waiting for transfers between devices: 84.9 us -> none  [local(): pre_act = lax.psum(pre_part, 'tp')]
    pallas_call x0 -> x1, Pallas kernels: none -> 65.5 us  [local(): pl.pallas_call(kernel, out_shape=(jax.ShapeDtypeStruct((1, TOKENS, WIDTH)...]
    psum x2 -> x0, blocking collectives: 57.5 us -> none  [the longest x1 35.2 us: local(): squares = lax.psum(jnp.sum(inputs * inputs, axis=1), 'tp')]
    select_n x33 -> x0, other arithmetic: 39.6 us -> none  [the longest x32 39.6 us: hop(): return jnp.where(reached, new, before)]
    transpose x1 -> x0, local copies, waits for them, and re-layouts: 19 us -> none  [local(): jnp.einsum('tsj,std->jtd', mixing_low, streams, preferred_element_type=jn...]
    dot_general x8 -> x0, matrix products: 16.6 us -> none  [the longest x1 8.52 us: local(): jnp.einsum('std,jtd->tsj', streams, lax.all_gather(layer_outputs, 'sectio...]
  transfers between devices with their start and end apart: 4 -> 0, of which waited for: 4 -> 0; matrix products, arithmetic and copies ran while one was open for 14% -> 0% of each run, Pallas kernels for 0% -> 0%
where the time goes in v1:
time: 75.9 us; the launch traced here: 74.7 us
  Pallas kernels  65.5 us (86%)
  local copies, waits for them, and re-layouts  8.48 us (11%)
    pallas_call x1, Pallas kernels, local(): pl.pallas_call(kernel, out_shape=(jax.ShapeDtypeStruct((1, TOKENS, WIDTH)...  65.5 us
    unnamed x13, local copies, waits for them, and re-layouts  7.69 us

profile of v1, /device:TPU:1, one launch (start us, length us, event | category | flops | bytes accessed | tf_op | source)
XLA Modules:
  0.0 74.7 jit_solution(4661611385959513870)
XLA Ops:
  0.6 1.0 %copy.9.w2_ref = bf16[1,384,96]{2,1,0:T(8,128)(2,1)S(1)} copy(bf16[1,384,96]{1,2,0:T(8,128)(2,1)} %param.11) | data formatting | bytes 147456 | tf_op args[5]
  1.6 0.0 copy-start
  1.6 1.1 %copy-done = bf16[1,3,128,1024]{3,2,1,0:T(8,128)(2,1)S(1)} copy-done((bf16[1,3,128,1024]{3,2,1,0:T(8,128)(2,1)S(1)}, bf16[1,3,128,1024]{3,2,1,0:T(8,128)(2,1)}, u32[]{:S(2)}) %copy-start) | copy-done | bytes 786456
  2.8 0.0 copy-start.1
  2.8 1.1 %copy-done.1 = bf16[1,1024,384]{2,1,0:T(8,128)(2,1)S(1)} copy-done((bf16[1,1024,384]{2,1,0:T(8,128)(2,1)S(1)}, bf16[1,1024,384]{2,1,0:T(8,128)(2,1)}, u32[]{:S(2)}) %copy-start.1) | copy-done | bytes 786456
  3.9 0.0 copy-start.2
  3.9 0.9 %copy-done.2 = bf16[1,128,1024]{2,1,0:T(8,128)(2,1)S(1)} copy-done((bf16[1,128,1024]{2,1,0:T(8,128)(2,1)S(1)}, bf16[1,128,1024]{2,1,0:T(8,128)(2,1)}, u32[]{:S(2)}) %copy-start.2) | copy-done | bytes 262168
  4.9 0.0 copy-start.3
  4.9 0.9 %copy-done.3 = bf16[1,128,1024]{2,1,0:T(8,128)(2,1)S(1)} copy-done((bf16[1,128,1024]{2,1,0:T(8,128)(2,1)S(1)}, bf16[1,128,1024]{2,1,0:T(8,128)(2,1)}, u32[]{:S(2)}) %copy-start.3) | copy-done | bytes 262168
  5.8 0.0 copy-start.4
  5.8 0.7 copy-done.4
  6.5 65.5 %shard_map.85 = (bf16[1,128,1024]{2,1,0:T(8,128)(2,1)S(1)}, f32[1,1024,384]{2,1,0:T(8,128)S(1)}, f32[1,384,96]{2,1,0:T(8,128)S(1)}) custom-call(bf16[1,128,1024]{2,1,0:T(8,128)(2,1)S(1)} %copy-done.2, bf16[1,3,128,1024]{3,2,1,0:T(8,128)(2,1)S(1)} %copy-done, bf16[1,128,1024]{2,1,0:T(8,128)(2,1)S(1)} %copy-done.3, bf16[1,1024]{1,0:T(2,128)(2,1)S(1)} %copy-done.4, ...), custom_call_target="tpu_custom_call" | custom-call | tf_op jit(solution)/shard_map/pallas_call | solution.py:355
  72.0 0.8 %copy.10 = f32[1,384,96]{1,2,0:T(8,128)} copy(f32[1,384,96]{2,1,0:T(8,128)S(1)} %get-tuple-element.5) | data formatting | bytes 294912 | tf_op jit(solution)/shard_map/pallas_call | solution.py:355
  72.8 0.7 copy.13
  73.5 1.1 %copy.14 = f32[1,1024,384]{2,1,0:T(8,128)} copy(f32[1,1024,384]{2,1,0:T(8,128)S(1)} %get-tuple-element.10) | data formatting | bytes 3145728
Async XLA Ops:
  1.6 1.1 %copy-start = (bf16[1,3,128,1024]{3,2,1,0:T(8,128)(2,1)S(1)}, bf16[1,3,128,1024]{3,2,1,0:T(8,128)(2,1)}, u32[]{:S(2)}) copy-start(bf16[1,3,128,1024]{3,2,1,0:T(8,128)(2,1)} %g_hbm.1) | copy-start | bytes 2359300
  2.8 1.1 %copy-start.1 = (bf16[1,1024,384]{2,1,0:T(8,128)(2,1)S(1)}, bf16[1,1024,384]{2,1,0:T(8,128)(2,1)}, u32[]{:S(2)}) copy-start(bf16[1,1024,384]{2,1,0:T(8,128)(2,1)} %w1_hbm.1) | copy-start | bytes 2359300
  3.9 0.9 %copy-start.2 = (bf16[1,128,1024]{2,1,0:T(8,128)(2,1)S(1)}, bf16[1,128,1024]{2,1,0:T(8,128)(2,1)}, u32[]{:S(2)}) copy-start(bf16[1,128,1024]{2,1,0:T(8,128)(2,1)} %x_hbm.1) | copy-start | bytes 786436
  4.9 0.9 %copy-start.3 = (bf16[1,128,1024]{2,1,0:T(8,128)(2,1)S(1)}, bf16[1,128,1024]{2,1,0:T(8,128)(2,1)}, u32[]{:S(2)}) copy-start(bf16[1,128,1024]{2,1,0:T(8,128)(2,1)} %r_hbm.1) | copy-start | bytes 786436
  5.8 0.7 copy-start.4

commit v2 on v0

v2 whole, which is shorter than its diff:
```python
import functools

import jax
import jax.numpy as jnp
from jax import lax
from jax.experimental import pallas as pl
from jax.experimental.pallas import tpu as pltpu
from jax.sharding import PartitionSpec as P

MESH = pl.DeviceIdType.MESH
F32, BF16 = jnp.float32, jnp.bfloat16
SECTIONS, SHARDS = 32, 8
PLANES, PLACES = 8, 4
TOKENS, WIDTH, HIDDEN = 128, 1024, 384
FULL_WIDTH = WIDTH * SHARDS
C0, C1 = 0.7978845608028654, 0.044715
FAR = [(4, q) for q in range(PLACES)]
MIDDLE = [(z, q) for q in range(PLACES) for z in (3, 5)]
CLOSE = [(z, q) for q in range(PLACES) for z in (2, 6)]
NEXT = [(z, q) for q in range(PLACES) for z in (1, 7)] + [(0, q) for q in range(1, PLACES)]
ALL = FAR + MIDDLE + CLOSE + NEXT


def dot(a, b):
    return jnp.dot(a, b, preferred_element_type=F32)


def dot_nt(a, b):
    return lax.dot_general(a, b, (((1,), (1,)), ((), ())), preferred_element_type=F32)


def dot_tn(a, b):
    return lax.dot_general(a, b, (((0,), (0,)), ((), ())), preferred_element_type=F32)


def halves(v):
    high = v.astype(BF16)
    return high, (v - high.astype(F32)).astype(BF16)


def grid(rows, columns):
    return (
        lax.broadcasted_iota(jnp.int32, (rows, columns), 0),
        lax.broadcasted_iota(jnp.int32, (rows, columns), 1),
    )


def pick(condition):
    return jnp.where(condition, 1.0, 0.0).astype(BF16)


def kernel(
    x_hbm, g_hbm, r_hbm, gain_hbm, w1_hbm, w2_hbm,
    out_v, first_v, second_v,
    stage, r_stage, gain_v, w1, w2, spread_m, sel_m, fold_m, normed_t,
    sent, held, r_sent, r_held, c_sent, c_held, s_sent, s_held, w_sent, w_held, o_sent, o_held,
    z_sent, z_held, act, d_sent, d_held, e_sent, e_held,
    in_sem, x_ss, x_rs, w_ss, w_rs, o_ss, o_rs, s_ss, s_rs,
    z_ss, z_rs, a_ss, a_rs, d_ss, d_rs, r_ss, r_rs, c_ss, c_rs, e_ss, e_rs,
):
    me = lax.axis_index("section")
    part = lax.axis_index("tp")
    plane, place = me >> 2, me & 3


    def section(offset):
        return ((plane + offset[0]) & 7) * PLACES + (place ^ offset[1])

    loads = []
    for b in range(2):
        rows = pl.ds(64 * b, 64)
        for s in range(3):
            loads.append((g_hbm.at[0, s, rows], stage.at[b, s]))
        loads.append((x_hbm.at[0, rows], stage.at[b, 3]))
    loads += [(gain_hbm, gain_v), (w1_hbm.at[0], w1)]
    for b in range(2):
        for f in range(4):
            loads.append((r_hbm.at[0, pl.ds(64 * b, 64), pl.ds(256 * f, 256)], r_stage.at[b, f]))
    loads.append((w2_hbm.at[0], w2.at[pl.ds(0, 96)]))
    loads = [pltpu.make_async_copy(src, dst, in_sem.at[n]) for n, (src, dst) in enumerate(loads)]
    for load in loads[:8]:
        load.start()

    barrier = pltpu.get_barrier_semaphore()

    def greet(device):
        pl.semaphore_signal(barrier, inc=1, device_id=device, device_id_type=MESH)

    for offset in ALL:
        greet({"section": section(offset)})
    for n in range(1, SHARDS):
        greet({"tp": part ^ n})
    for load in loads[8:]:
        load.start()

    class Exchange:
        def __init__(self, peers, here, device, block, landing, ss, rs):
            self.peers, self.here = peers, here

            def copy(to, slot):
                return pltpu.make_async_remote_copy(
                    src_ref=block(to), dst_ref=landing(slot), send_sem=ss.at[to], recv_sem=rs.at[slot],
                    device_id=device(to), device_id_type=MESH,
                )

            self.copy = copy

        def send(self, peers=None):
            for to in peers or self.peers:
                self.copy(to, self.here).start()

        def receive(self):
            for to in self.peers:
                self.copy(to, to).wait_recv()

        def drain(self):
            for to in self.peers:
                self.copy(to, self.here).wait_send()

    by_section = lambda to: {"section": to}
    by_part = lambda to: {"tp": to}
    by_place = lambda to: {"section": plane * PLACES + to}
    by_plane = lambda to: {"section": to * PLACES + place}
    far, middle, close, beside = ([section(offset) for offset in group] for group in (FAR, MIDDLE, CLOSE, NEXT))
    sections = far + middle + close + beside
    parts = [part ^ n for n in range(1, SHARDS)]
    places = [place ^ n for n in range(1, PLACES)]
    planes = [(plane + n) & 7 for n in (4, 3, 5, 2, 6, 1, 7)]
    xg = Exchange(sections, me, by_section, lambda p: sent.at[p], lambda p: held.at[p], x_ss, x_rs)
    wx = Exchange(sections, me, by_section, lambda p: w_sent.at[p], lambda p: w_held.at[p], w_ss, w_rs)
    ox = Exchange(sections, me, by_section, lambda p: o_sent.at[p], lambda p: o_held.at[p], o_ss, o_rs)
    zx = Exchange(parts, part, by_part, lambda p: z_sent.at[p], lambda p: z_held.at[p], z_ss, z_rs)
    ax = Exchange(parts, part, by_part, lambda p: act.at[part], lambda p: act.at[p], a_ss, a_rs)
    dx = Exchange(parts, part, by_part, lambda p: d_sent.at[p], lambda p: d_held.at[p], d_ss, d_rs)
    rx = Exchange(places, place, by_place, lambda p: r_sent.at[:, p], lambda p: r_held.at[p], r_ss, r_rs)
    cx = Exchange(places, place, by_place, lambda p: c_sent.at[p], lambda p: c_held.at[:, p], c_ss, c_rs)
    sx = Exchange(planes, plane, by_plane, lambda p: s_sent.at[p], lambda p: s_held.at[p], s_ss, s_rs)

    row, col = grid(256, 256)
    regroup = pick(((row >> 2) & 3) * 64 + (row >> 4) * 4 + (row & 3) == col)

    for b in range(2):
        for load in loads[4 * b : 4 * b + 4]:
            load.wait()
        grouped = dot(regroup, stage[b].reshape(256, WIDTH)).astype(BF16)
        sent[pl.ds(16 * b, 16)] = grouped.reshape(16, 16, WIDTH)
    pl.semaphore_wait(barrier, SECTIONS - 1 + SHARDS - 1)
    xg.send(far)
    held[pl.ds(me, 1)] = sent[pl.ds(me, 1)]

    loads[8].wait()
    loads[9].wait()
    gain = gain_v[...].astype(F32)
    x = jnp.concatenate([stage[0, 3], stage[1, 3]], axis=0).astype(F32)
    product = dot(jnp.concatenate(halves(x * gain), axis=0), w1[...])
    squares = jnp.broadcast_to(jnp.sum(x * x, axis=1, keepdims=True), (TOKENS, 128))
    z_sent[...] = jnp.concatenate([product[:TOKENS] + product[TOKENS:], squares], axis=1).reshape(SHARDS, 16, 512)
    zx.send()
    xg.send(middle)
    z_held[pl.ds(part, 1)] = z_sent[pl.ds(part, 1)]

    for load in loads[10:]:
        load.wait()
    for b in range(2):
        grouped = dot(regroup, r_stage[b].reshape(256, 256)).astype(BF16)
        r_sent[pl.ds(4 * b, 4)] = grouped.reshape(4, PLACES, 16, 256)
    rx.send()
    r_held[pl.ds(place, 1)] = r_sent[:, pl.ds(place, 1)].reshape(1, PLANES, 16, 256)

    zx.receive()
    total = z_held[0]
    for p in range(1, SHARDS):
        total = total + z_held[p]
    scale = lax.rsqrt(total[:, HIDDEN:] / FULL_WIDTH + 1e-05)
    own = jnp.concatenate([total[:, :HIDDEN] * scale[:, :1], scale], axis=1)
    act[pl.ds(part, 1)] = own.reshape(1, 16, 512)
    ax.send()
    xg.send(close)

    rx.receive()
    running = jnp.zeros((PLANES, 16, 256), F32)
    for p in reversed(range(PLACES)):
        running = running + r_held[p].astype(F32)
        c_sent[p] = running.astype(BF16)
    s_sent[...] = running.astype(BF16)
    c_held[:, pl.ds(place, 1)] = c_sent[pl.ds(place, 1)].reshape(PLANES, 1, 16, 256)
    s_held[pl.ds(plane, 1)] = s_sent[pl.ds(plane, 1)]
    cx.send()

    w2[pl.ds(96, 32)] = jnp.zeros((32, HIDDEN), BF16)
    ax.receive()
    pre = act[:, :, :HIDDEN].reshape(TOKENS, HIDDEN)
    inverse = act[:, :, HIDDEN:].reshape(TOKENS, 128)[:, :1]
    square = pre * pre
    bend = jnp.tanh(C0 * pre * (1.0 + C1 * square))
    hidden = 0.5 * pre * (1.0 + bend)
    slope = 0.5 * (1.0 + bend) + 0.5 * pre * (1.0 - bend * bend) * (C0 * (1.0 + 3.0 * C1 * square))
    h_high, h_low = halves(hidden)
    mixing = dot_nt(h_high, w2[...]) + dot_nt(h_low, w2[...])
    row, col = grid(TOKENS, 128)
    mixing = jnp.where((col & 31) <= me, mixing, 0.0)
    w_sent[...] = mixing.reshape(SECTIONS, 4, 128)
    w_held[pl.ds(me, 1)] = w_sent[pl.ds(me, 1)]
    wx.send()
    xg.send(beside)
    sx.send()

    row, col = grid(128, 512)
    sel_m[...] = pick((row >> 2) * 16 + 12 + (row & 3) == col)
    fold_m[...] = pick((((row >> 2) & 3) * SHARDS + (row >> 4) == (col >> 4)) & ((row & 3) == (col & 3)))
    row, col = grid(512, 128)
    spread_m[...] = pick(((row >> 4) == (col >> 2)) & ((row & 3) == (col & 3)))
    for b in range(2):
        x = stage[b, 3].astype(F32)
        normed = (x * inverse[64 * b : 64 * b + 64] * gain).astype(BF16)
        normed_t[:, pl.ds(64 * b, 64)] = normed.T

    xg.receive()
    table = held[...].reshape(512, WIDTH)
    streams = dot(sel_m[...], table).astype(BF16)
    gram = dot_nt(table, streams)
    row, col = grid(512, 128)
    gram = jnp.where((row & 3) == (col & 3), gram, 0.0)
    rr, cc = grid(128, 128)
    across = pick((rr >> 2) == (cc & 31))
    high, low = halves(gram)
    wide = dot(high, across) + dot(low, across)
    which = (row >> 2) & 3
    wide = jnp.where((which == (col >> 5)) & (which < 3) & ((col & 31) <= (row >> 4)), wide, 0.0)
    high, low = halves(wide)
    d_sent[...] = (dot(fold_m[...], high) + dot(fold_m[...], low)).reshape(SHARDS, 16, 128)
    dx.send()
    d_held[pl.ds(part, 1)] = d_sent[pl.ds(part, 1)]

    wx.receive()
    row, col = grid(128, 512)
    mixing = w_held[...].reshape(128, 128).astype(BF16)
    mixing = dot(mixing, pick(((row >> 5) == (col >> 7)) & ((row & 31) == ((col >> 2) & 31)))).astype(BF16)
    mixing = dot(spread_m[...], mixing)
    row, col = grid(512, 512)
    mixing = jnp.where((((row >> 2) & 3) == (col >> 7)) & ((row & 3) == (col & 3)), mixing, 0.0)
    weights = mixing[:, :128] + mixing[:, 128:256] + mixing[:, 256:384]
    weights = weights.astype(BF16).T
    partial = [dot(weights, table[:, 256 * f : 256 * f + 256]) for f in range(4)]
    sx.receive()
    running = jnp.zeros((16, 256), F32)
    carried = [None] * PLANES
    for p in reversed(range(PLANES)):
        carried[p] = jnp.concatenate([running] * PLACES, axis=0)
        running = running + s_held[p].astype(F32)
    for b in range(2):
        stacked = jnp.concatenate([p[64 * b : 64 * b + 64] for p in partial], axis=0)
        high, low = halves(stacked)
        block = dot(regroup, high) + dot(regroup, low) + jnp.concatenate(carried[4 * b : 4 * b + 4], axis=0)
        o_sent[pl.ds(16 * b, 16)] = block.astype(BF16).reshape(16, 16, 256)
    o_held[pl.ds(me, 1)] = o_sent[pl.ds(me, 1)]

    ox.send(far + middle)
    dx.receive()
    total = d_held[0]
    for p in range(1, SHARDS):
        total = total + d_held[p]
    for a in range(4):
        e_sent[a] = total[4 * a : 4 * a + 4]

    home, turn = me & 7, me >> 3

    def e_copy(a, b):
        return pltpu.make_async_remote_copy(
            src_ref=e_sent.at[a], dst_ref=e_held.at[me], send_sem=e_ss.at[a, b], recv_sem=e_rs.at[me],
            device_id={"section": SHARDS * a + part, "tp": b}, device_id_type=MESH,
        )

    def e_each(do):
        for n in range(1, SHARDS):
            for a in range(4):
                do(e_copy((turn + a) & 3, part ^ n))
        for a in range(4):

            @pl.when((home != part) | (turn != a))
            def _():
                do(e_copy(a, part))

    def e_receive(n):
        pltpu.make_async_remote_copy(
            src_ref=e_sent.at[0], dst_ref=e_held.at[n], send_sem=e_ss.at[0, 0], recv_sem=e_rs.at[n],
            device_id={"section": n, "tp": home}, device_id_type=MESH,
        ).wait_recv()

    e_each(lambda copy: copy.start())
    ox.send(close + beside)

    @pl.when(home == part)
    def _():
        e_held[pl.ds(me, 1)] = e_sent[pl.ds(turn, 1)]

    cx.receive()
    near = [dot_tn(regroup, c_held[pl.ds(4 * b, 4)].reshape(256, 256)) for b in range(2)]
    for exchange in (zx, ax, rx, cx, sx, xg, wx, dx):
        exchange.drain()

    for n in sections:
        e_receive(n)

    @pl.when(home != part)
    def _():
        e_receive(me)

    mix_grad = e_held[...].reshape(TOKENS, 128)
    g_high, g_low = halves(mix_grad)
    pre_grad = ((dot(g_high, w2[...]) + dot(g_low, w2[...])) * slope).astype(BF16)
    first_v[0] = dot(normed_t[...], pre_grad)
    second = dot_tn(g_high, h_high) + dot_tn(g_low, h_high) + dot_tn(g_high, h_low)
    second_v[0] = second[:96]
    along = jnp.sum(pre_grad.astype(F32) * pre, axis=1, keepdims=True)
    inner = inverse * inverse * along / FULL_WIDTH
    local = inverse * (dot_nt(pre_grad, w1[...]) * gain)

    ox.receive()
    for b in range(2):
        rows = slice(64 * b, 64 * b + 64)
        arrived = dot_tn(regroup, o_held[pl.ds(16 * b, 16)].reshape(256, 256)) + near[b]
        x = stage[b, 3].astype(F32)
        for f in range(4):
            lanes = slice(256 * f, 256 * f + 256)
            value = arrived[64 * f : 64 * f + 64] + (local[rows, lanes] - x[:, lanes] * inner[rows])
            out_v[0, pl.ds(64 * b, 64), pl.ds(256 * f, 256)] = value.astype(BF16)

    ox.drain()
    e_each(lambda copy: copy.wait_send())


def local(layer_outputs, stream_grads, residual_grads, norm_gain, first_weight, second_weight):
    hbm = pl.BlockSpec(memory_space=pltpu.HBM)
    vmem = pl.BlockSpec(memory_space=pltpu.VMEM)
    dma = pltpu.SemaphoreType.DMA
    by_section = lambda rows, lanes, dtype: pltpu.VMEM((SECTIONS, rows, lanes), dtype)
    by_part = lambda rows, lanes: pltpu.VMEM((SHARDS, rows, lanes), F32)
    by_place = lambda *lead: pltpu.VMEM((*lead, 16, 256), BF16)
    shapes = (
        jax.ShapeDtypeStruct((1, TOKENS, WIDTH), BF16),
        jax.ShapeDtypeStruct((1, WIDTH, HIDDEN), F32),
        jax.ShapeDtypeStruct((1, 96, HIDDEN), F32),
    )
    args = (layer_outputs, stream_grads, residual_grads, norm_gain, first_weight, jnp.swapaxes(second_weight, 1, 2))
    grads = pl.pallas_call(
        kernel,
        out_shape=shapes,
        in_specs=[hbm] * 6,
        out_specs=(vmem, vmem, vmem),
        scratch_shapes=[
            pltpu.VMEM((2, 4, 64, WIDTH), BF16),
            pltpu.VMEM((2, 4, 64, 256), BF16),
            pltpu.VMEM((1, WIDTH), BF16),
            pltpu.VMEM((WIDTH, HIDDEN), BF16),
            pltpu.VMEM((128, HIDDEN), BF16),
            pltpu.VMEM((512, 128), BF16),
            pltpu.VMEM((128, 512), BF16),
            pltpu.VMEM((128, 512), BF16),
            pltpu.VMEM((WIDTH, TOKENS), BF16),
            by_section(16, WIDTH, BF16), by_section(16, WIDTH, BF16),
            by_place(PLANES, PLACES), by_place(PLACES, PLANES),
            by_place(PLACES, PLANES), by_place(PLANES, PLACES),
            by_place(PLANES), by_place(PLANES),
            by_section(4, 128, F32), by_section(4, 128, F32),
            by_section(16, 256, BF16), by_section(16, 256, BF16),
            by_part(16, 512), by_part(16, 512), by_part(16, 512),
            by_part(16, 128), by_part(16, 128),
            pltpu.VMEM((4, 4, 128), F32),
            by_section(4, 128, F32),
            dma((19,)),
            *[dma((SECTIONS,)) for _ in range(6)],
            *[dma((PLANES,)) for _ in range(2)],
            *[dma((SHARDS,)) for _ in range(6)],
            *[dma((PLACES,)) for _ in range(4)],
            dma((4, SHARDS)), dma((SECTIONS,)),
        ],
        compiler_params=pltpu.CompilerParams(
            collective_id=0, has_side_effects=True, vmem_limit_bytes=32 * 1024 * 1024
        ),
    )(*[pltpu.with_memory_space_constraint(a, pltpu.HBM) for a in args])
    return grads[0], grads[1], jnp.swapaxes(grads[2], 1, 2)


def solution(mesh):
    placed = (
        P("section", None, "tp"),
        P("section", None, None, "tp"),
        P("section", None, "tp"),
        P("section", "tp"),
        P("section", "tp", None),
        P("section", None, None),
    )
    return jax.shard_map(
        local,
        mesh=mesh,
        in_specs=placed,
        out_specs=(P("section", None, "tp"), P("section", "tp", None), P("section", None, None)),
        check_vma=False,
    )
```

time: 496 us -> 59 us (0.12)
  waiting for transfers between devices: 343 us -> 0 us
  blocking collectives: 57.5 us -> 0 us
  Pallas kernels: 0 us -> 55.7 us
  other arithmetic: 43.5 us -> 0 us
  local copies, waits for them, and re-layouts: 19.3 us -> 2.51 us
  matrix products: 16.6 us -> 0 us
  between operations: 13.9 us -> 0.64 us
    all_gather x2 -> x0, waiting for transfers between devices: 132 us -> none  [the longest x1 76.7 us: local(): lax.all_gather(layer_outputs, 'section', axis=0, tiled=True)]
    reduce_scatter x1 -> x0, waiting for transfers between devices: 125 us -> none  [local(): summed = lax.psum_scatter(block, 'section', scatter_dimension=0, tiled=True)]
    psum x1 -> x0, waiting for transfers between devices: 84.9 us -> none  [local(): pre_act = lax.psum(pre_part, 'tp')]
    psum x2 -> x0, blocking collectives: 57.5 us -> none  [the longest x1 35.2 us: local(): squares = lax.psum(jnp.sum(inputs * inputs, axis=1), 'tp')]
    pallas_call x0 -> x1, Pallas kernels: none -> 55.7 us  [local(): pl.pallas_call(kernel, out_shape=shapes, in_specs=[hbm] * 6, out_specs=(v...]
    select_n x33 -> x0, other arithmetic: 39.6 us -> none  [the longest x32 39.6 us: hop(): return jnp.where(reached, new, before)]
    transpose x1 -> x0, local copies, waits for them, and re-layouts: 19 us -> none  [local(): jnp.einsum('tsj,std->jtd', mixing_low, streams, preferred_element_type=jn...]
    dot_general x8 -> x0, matrix products: 16.6 us -> none  [the longest x1 8.52 us: local(): jnp.einsum('std,jtd->tsj', streams, lax.all_gather(layer_outputs, 'sectio...]
  transfers between devices with their start and end apart: 4 -> 0, of which waited for: 4 -> 0; matrix products, arithmetic and copies ran while one was open for 14% -> 0% of each run, Pallas kernels for 0% -> 0%
where the time goes in v2:
time: 59 us; the launch traced here: 58.9 us
  Pallas kernels  55.7 us (94%)
  local copies, waits for them, and re-layouts  2.51 us (4%)
  between operations  0.64 us (1%)
    pallas_call x1, Pallas kernels, local(): pl.pallas_call(kernel, out_shape=shapes, in_specs=[hbm] * 6, out_specs=(v...  55.7 us
    unnamed x3, local copies, waits for them, and re-layouts  2.51 us

profile of v2, /device:TPU:1, one launch (start us, length us, event | category | flops | bytes accessed | tf_op | source)
XLA Modules:
  0.0 58.9 jit_solution(5538676598946042281)
XLA Ops:
  0.6 55.7 %shard_map.85 = (bf16[1,128,1024]{2,1,0:T(8,128)(2,1)S(1)}, f32[1,1024,384]{2,1,0:T(8,128)S(1)}, f32[1,96,384]{2,1,0:T(8,128)S(1)}) custom-call(bf16[1,128,1024]{2,1,0:T(8,128)(2,1)} %x_hbm.1, bf16[1,3,128,1024]{3,2,1,0:T(8,128)(2,1)} %g_hbm.1, bf16[1,128,1024]{2,1,0:T(8,128)(2,1)} %r_hbm.1, bf16[1,1024]{1,0:T(2,128)(2,1)} %gain_hbm.1, ...), custom_call_target="tpu_custom_call" | custom-call | tf_op jit(solution)/shard_map/pallas_call | solution.py:346
  56.4 0.7 %copy.12 = bf16[1,128,1024]{2,1,0:T(8,128)(2,1)} copy(bf16[1,128,1024]{2,1,0:T(8,128)(2,1)S(1)} %get-tuple-element.12) | data formatting | bytes 524288
  57.1 1.1 %copy.13 = f32[1,1024,384]{2,1,0:T(8,128)} copy(f32[1,1024,384]{2,1,0:T(8,128)S(1)} %get-tuple-element.13) | data formatting | bytes 3145728
  58.2 0.7 %copy.14 = f32[1,384,96]{1,2,0:T(8,128)} copy(f32[1,384,96]{1,2,0:T(8,128)S(1)} %bitcast.2) | data formatting | bytes 294912

commit v3 on v2

--- a/solution.py
+++ b/solution.py
@@ -19,6 +19,7 @@
 CLOSE = [(z, q) for q in range(PLACES) for z in (2, 6)]
 NEXT = [(z, q) for q in range(PLACES) for z in (1, 7)] + [(0, q) for q in range(1, PLACES)]
 ALL = FAR + MIDDLE + CLOSE + NEXT
+AROUND = (5, 7, 3, 4, 1, 6, 2)
 
 
 def dot(a, b):
@@ -52,7 +53,7 @@
 def kernel(
     x_hbm, g_hbm, r_hbm, gain_hbm, w1_hbm, w2_hbm,
     out_v, first_v, second_v,
-    stage, r_stage, gain_v, w1, w2, spread_m, sel_m, fold_m, normed_t,
+    stage, r_stage, gain_v, w1, w2, spread_m, sel_m, fold_m, across_m, wide_m, same_m, kept_m, ungroup_m, normed_t,
     sent, held, r_sent, r_held, c_sent, c_held, s_sent, s_held, w_sent, w_held, o_sent, o_held,
     z_sent, z_held, act, d_sent, d_held, e_sent, e_held,
     in_sem, x_ss, x_rs, w_ss, w_rs, o_ss, o_rs, s_ss, s_rs,
@@ -123,7 +124,7 @@
     by_plane = lambda to: {"section": to * PLACES + place}
     far, middle, close, beside = ([section(offset) for offset in group] for group in (FAR, MIDDLE, CLOSE, NEXT))
     sections = far + middle + close + beside
-    parts = [part ^ n for n in range(1, SHARDS)]
+    parts = [part ^ n for n in AROUND]
     places = [place ^ n for n in range(1, PLACES)]
     planes = [(plane + n) & 7 for n in (4, 3, 5, 2, 6, 1, 7)]
     xg = Exchange(sections, me, by_section, lambda p: sent.at[p], lambda p: held.at[p], x_ss, x_rs)
@@ -144,10 +145,6 @@
             load.wait()
         grouped = dot(regroup, stage[b].reshape(256, WIDTH)).astype(BF16)
         sent[pl.ds(16 * b, 16)] = grouped.reshape(16, 16, WIDTH)
-    pl.semaphore_wait(barrier, SECTIONS - 1 + SHARDS - 1)
-    xg.send(far)
-    held[pl.ds(me, 1)] = sent[pl.ds(me, 1)]
-
     loads[8].wait()
     loads[9].wait()
     gain = gain_v[...].astype(F32)
@@ -155,9 +152,12 @@
     product = dot(jnp.concatenate(halves(x * gain), axis=0), w1[...])
     squares = jnp.broadcast_to(jnp.sum(x * x, axis=1, keepdims=True), (TOKENS, 128))
     z_sent[...] = jnp.concatenate([product[:TOKENS] + product[TOKENS:], squares], axis=1).reshape(SHARDS, 16, 512)
+
+    pl.semaphore_wait(barrier, SECTIONS - 1 + SHARDS - 1)
     zx.send()
-    xg.send(middle)
     z_held[pl.ds(part, 1)] = z_sent[pl.ds(part, 1)]
+    xg.send(far + middle)
+    held[pl.ds(me, 1)] = sent[pl.ds(me, 1)]
 
     for load in loads[10:]:
         load.wait()
@@ -175,7 +175,7 @@
     own = jnp.concatenate([total[:, :HIDDEN] * scale[:, :1], scale], axis=1)
     act[pl.ds(part, 1)] = own.reshape(1, 16, 512)
     ax.send()
-    xg.send(close)
+    xg.send(close + beside)
 
     rx.receive()
     running = jnp.zeros((PLANES, 16, 256), F32)
@@ -202,14 +202,22 @@
     w_sent[...] = mixing.reshape(SECTIONS, 4, 128)
     w_held[pl.ds(me, 1)] = w_sent[pl.ds(me, 1)]
     wx.send()
-    xg.send(beside)
     sx.send()
 
     row, col = grid(128, 512)
     sel_m[...] = pick((row >> 2) * 16 + 12 + (row & 3) == col)
     fold_m[...] = pick((((row >> 2) & 3) * SHARDS + (row >> 4) == (col >> 4)) & ((row & 3) == (col & 3)))
+    wide_m[...] = pick(((row >> 5) == (col >> 7)) & ((row & 31) == ((col >> 2) & 31)))
     row, col = grid(512, 128)
-    spread_m[...] = pick(((row >> 4) == (col >> 2)) & ((row & 3) == (col & 3)))
+    same = (row & 3) == (col & 3)
+    spread_m[...] = pick(((row >> 4) == (col >> 2)) & same)
+    same_m[...] = jnp.where(same, 1.0, 0.0)
+    which = (row >> 2) & 3
+    kept_m[...] = jnp.where((which == (col >> 5)) & (which < 3) & ((col & 31) <= (row >> 4)), 1.0, 0.0)
+    row, col = grid(128, 128)
+    across_m[...] = pick((row >> 2) == (col & 31))
+    row, col = grid(256, 256)
+    ungroup_m[...] = pick(((col >> 2) & 3) * 64 + (col >> 4) * 4 + (col & 3) == row)
     for b in range(2):
         x = stage[b, 3].astype(F32)
         normed = (x * inverse[64 * b : 64 * b + 64] * gain).astype(BF16)
@@ -219,27 +227,20 @@
     table = held[...].reshape(512, WIDTH)
     streams = dot(sel_m[...], table).astype(BF16)
     gram = dot_nt(table, streams)
-    row, col = grid(512, 128)
-    gram = jnp.where((row & 3) == (col & 3), gram, 0.0)
-    rr, cc = grid(128, 128)
-    across = pick((rr >> 2) == (cc & 31))
-    high, low = halves(gram)
-    wide = dot(high, across) + dot(low, across)
-    which = (row >> 2) & 3
-    wide = jnp.where((which == (col >> 5)) & (which < 3) & ((col & 31) <= (row >> 4)), wide, 0.0)
+    high, low = halves(gram * same_m[...])
+    wide = (dot(high, across_m[...]) + dot(low, across_m[...])) * kept_m[...]
     high, low = halves(wide)
     d_sent[...] = (dot(fold_m[...], high) + dot(fold_m[...], low)).reshape(SHARDS, 16, 128)
     dx.send()
     d_held[pl.ds(part, 1)] = d_sent[pl.ds(part, 1)]
 
     wx.receive()
-    row, col = grid(128, 512)
     mixing = w_held[...].reshape(128, 128).astype(BF16)
-    mixing = dot(mixing, pick(((row >> 5) == (col >> 7)) & ((row & 31) == ((col >> 2) & 31)))).astype(BF16)
-    mixing = dot(spread_m[...], mixing)
-    row, col = grid(512, 512)
-    mixing = jnp.where((((row >> 2) & 3) == (col >> 7)) & ((row & 3) == (col & 3)), mixing, 0.0)
-    weights = mixing[:, :128] + mixing[:, 128:256] + mixing[:, 256:384]
+    mixing = dot(spread_m[...], dot(mixing, wide_m[...]).astype(BF16))
+    row, col = grid(512, 128)
+    which = (row >> 2) & 3
+    weights = jnp.where(which == 0, mixing[:, :128], jnp.where(which == 1, mixing[:, 128:256], mixing[:, 256:384]))
+    weights = jnp.where(which < 3, weights * same_m[...], 0.0)
     weights = weights.astype(BF16).T
     partial = [dot(weights, table[:, 256 * f : 256 * f + 256]) for f in range(4)]
     sx.receive()
@@ -250,8 +251,7 @@
         running = running + s_held[p].astype(F32)
     for b in range(2):
         stacked = jnp.concatenate([p[64 * b : 64 * b + 64] for p in partial], axis=0)
-        high, low = halves(stacked)
-        block = dot(regroup, high) + dot(regroup, low) + jnp.concatenate(carried[4 * b : 4 * b + 4], axis=0)
+        block = dot(regroup, stacked.astype(BF16)) + jnp.concatenate(carried[4 * b : 4 * b + 4], axis=0)
         o_sent[pl.ds(16 * b, 16)] = block.astype(BF16).reshape(16, 16, 256)
     o_held[pl.ds(me, 1)] = o_sent[pl.ds(me, 1)]
 
@@ -272,8 +272,8 @@
         )
 
     def e_each(do):
-        for n in range(1, SHARDS):
-            for a in range(4):
+        for a in (2, 1, 3, 0):
+            for n in AROUND:
                 do(e_copy((turn + a) & 3, part ^ n))
         for a in range(4):
 
@@ -295,7 +295,7 @@
         e_held[pl.ds(me, 1)] = e_sent[pl.ds(turn, 1)]
 
     cx.receive()
-    near = [dot_tn(regroup, c_held[pl.ds(4 * b, 4)].reshape(256, 256)) for b in range(2)]
+    near = [dot(ungroup_m[...], c_held[pl.ds(4 * b, 4)].reshape(256, 256)) for b in range(2)]
     for exchange in (zx, ax, rx, cx, sx, xg, wx, dx):
         exchange.drain()
 
@@ -316,18 +316,26 @@
     inner = inverse * inverse * along / FULL_WIDTH
     local = inverse * (dot_nt(pre_grad, w1[...]) * gain)
 
+    e_each(lambda copy: copy.wait_send())
+    ox.drain()
     ox.receive()
     for b in range(2):
         rows = slice(64 * b, 64 * b + 64)
-        arrived = dot_tn(regroup, o_held[pl.ds(16 * b, 16)].reshape(256, 256)) + near[b]
+        arrived = dot(ungroup_m[...], o_held[pl.ds(16 * b, 16)].reshape(256, 256)) + near[b]
         x = stage[b, 3].astype(F32)
         for f in range(4):
             lanes = slice(256 * f, 256 * f + 256)
             value = arrived[64 * f : 64 * f + 64] + (local[rows, lanes] - x[:, lanes] * inner[rows])
             out_v[0, pl.ds(64 * b, 64), pl.ds(256 * f, 256)] = value.astype(BF16)
 
-    ox.drain()
-    e_each(lambda copy: copy.wait_send())
+
+def handover(out_in, first_in, second_in, out, first, second, sems):
+    pairs = ((first_in, first), (out_in, out), (second_in, second))
+    copies = [pltpu.make_async_copy(src, dst, sems.at[n]) for n, (src, dst) in enumerate(pairs)]
+    for copy in copies:
+        copy.start()
+    for copy in copies:
+        copy.wait()
 
 
 def local(layer_outputs, stream_grads, residual_grads, norm_gain, first_weight, second_weight):
@@ -357,6 +365,11 @@
             pltpu.VMEM((512, 128), BF16),
             pltpu.VMEM((128, 512), BF16),
             pltpu.VMEM((128, 512), BF16),
+            pltpu.VMEM((128, 128), BF16),
+            pltpu.VMEM((128, 512), BF16),
+            pltpu.VMEM((512, 128), F32),
+            pltpu.VMEM((512, 128), F32),
+            pltpu.VMEM((256, 256), BF16),
             pltpu.VMEM((WIDTH, TOKENS), BF16),
             by_section(16, WIDTH, BF16), by_section(16, WIDTH, BF16),
             by_place(PLANES, PLACES), by_place(PLACES, PLANES),
@@ -379,6 +392,14 @@
             collective_id=0, has_side_effects=True, vmem_limit_bytes=32 * 1024 * 1024
         ),
     )(*[pltpu.with_memory_space_constraint(a, pltpu.HBM) for a in args])
+    grads = pl.pallas_call(
+        handover,
+        out_shape=shapes,
+        in_specs=[vmem] * 3,
+        out_specs=(hbm,) * 3,
+        scratch_shapes=[dma((3,))],
+        compiler_params=pltpu.CompilerParams(vmem_limit_bytes=8 * 1024 * 1024),
+    )(*[pltpu.with_memory_space_constraint(g, pltpu.VMEM) for g in grads])
     return grads[0], grads[1], jnp.swapaxes(grads[2], 1, 2)
 
 

time: 59 us -> 56.2 us (0.953)
  local copies, waits for them, and re-layouts: 2.51 us -> 0 us
    unnamed x3 -> x0, local copies, waits for them, and re-layouts: 2.51 us -> none
    pallas_call x1, Pallas kernels: 55.7 us -> 54.1 us  [local(): pl.pallas_call(kernel, out_shape=shapes, in_specs=[hbm] * 6, out_specs=(v...]
    pallas_call x0 -> x1, Pallas kernels: none -> 1.29 us  [local(): pl.pallas_call(handover, out_shape=shapes, in_specs=[vmem] * 3, out_specs...]
where the time goes in v3:
time: 56.2 us; the launch traced here: 56 us
  Pallas kernels  55.4 us (99%)
  between operations  0.64 us (1%)
    pallas_call x1, Pallas kernels, local(): pl.pallas_call(kernel, out_shape=shapes, in_specs=[hbm] * 6, out_specs=(v...  54.1 us
    pallas_call x1, Pallas kernels, local(): pl.pallas_call(handover, out_shape=shapes, in_specs=[vmem] * 3, out_specs...  1.29 us

profile of v3, /device:TPU:1, one launch (start us, length us, event | category | flops | bytes accessed | tf_op | source)
XLA Modules:
  0.0 56.0 jit_solution(1934495581199729117)
XLA Ops:
  0.6 54.1 %shard_map.85 = (bf16[1,128,1024]{2,1,0:T(8,128)(2,1)S(1)}, f32[1,1024,384]{2,1,0:T(8,128)S(1)}, f32[1,96,384]{2,1,0:T(8,128)S(1)}) custom-call(bf16[1,128,1024]{2,1,0:T(8,128)(2,1)} %x_hbm.1, bf16[1,3,128,1024]{3,2,1,0:T(8,128)(2,1)} %g_hbm.1, bf16[1,128,1024]{2,1,0:T(8,128)(2,1)} %r_hbm.1, bf16[1,1024]{1,0:T(2,128)(2,1)} %gain_hbm.1, ...), custom_call_target="tpu_custom_call" | custom-call | tf_op jit(solution)/shard_map/pallas_call | solution.py:354
  54.8 1.3 %shard_map.86 = (bf16[1,128,1024]{2,1,0:T(8,128)(2,1)}, f32[1,1024,384]{2,1,0:T(8,128)}, f32[1,96,384]{2,1,0:T(8,128)}) custom-call(bf16[1,128,1024]{2,1,0:T(8,128)(2,1)S(1)} %get-tuple-element.9.out_in, f32[1,1024,384]{2,1,0:T(8,128)S(1)} %get-tuple-element.10.first_in, f32[1,96,384]{2,1,0:T(8,128)S(1)} %get-tuple-element.11.second_in), custom_call_target="tpu_custom_call" | custom-call | tf_op jit(solution)/shard_map/pallas_call | solution.py:395

commit v4 on v3

--- a/solution.py
+++ b/solution.py
@@ -14,8 +14,8 @@
 TOKENS, WIDTH, HIDDEN = 128, 1024, 384
 FULL_WIDTH = WIDTH * SHARDS
 C0, C1 = 0.7978845608028654, 0.044715
-FAR = [(4, q) for q in range(PLACES)]
-MIDDLE = [(z, q) for q in range(PLACES) for z in (3, 5)]
+FAR = [(4, q) for q in (2, 3, 0, 1)]
+MIDDLE = [(z, q) for q in (2, 3, 0, 1) for z in (3, 5)]
 CLOSE = [(z, q) for q in range(PLACES) for z in (2, 6)]
 NEXT = [(z, q) for q in range(PLACES) for z in (1, 7)] + [(0, q) for q in range(1, PLACES)]
 ALL = FAR + MIDDLE + CLOSE + NEXT
@@ -56,8 +56,7 @@
     stage, r_stage, gain_v, w1, w2, spread_m, sel_m, fold_m, across_m, wide_m, same_m, kept_m, ungroup_m, normed_t,
     sent, held, r_sent, r_held, c_sent, c_held, s_sent, s_held, w_sent, w_held, o_sent, o_held,
     z_sent, z_held, act, d_sent, d_held, e_sent, e_held,
-    in_sem, x_ss, x_rs, w_ss, w_rs, o_ss, o_rs, s_ss, s_rs,
-    z_ss, z_rs, a_ss, a_rs, d_ss, d_rs, r_ss, r_rs, c_ss, c_rs, e_ss, e_rs,
+    in_sem, sems,
 ):
     me = lax.axis_index("section")
     part = lax.axis_index("tp")
@@ -67,40 +66,52 @@
     def section(offset):
         return ((plane + offset[0]) & 7) * PLACES + (place ^ offset[1])
 
-    loads = []
-    for b in range(2):
-        rows = pl.ds(64 * b, 64)
-        for s in range(3):
-            loads.append((g_hbm.at[0, s, rows], stage.at[b, s]))
-        loads.append((x_hbm.at[0, rows], stage.at[b, 3]))
-    loads += [(gain_hbm, gain_v), (w1_hbm.at[0], w1)]
-    for b in range(2):
-        for f in range(4):
-            loads.append((r_hbm.at[0, pl.ds(64 * b, 64), pl.ds(256 * f, 256)], r_stage.at[b, f]))
-    loads.append((w2_hbm.at[0], w2.at[pl.ds(0, 96)]))
-    loads = [pltpu.make_async_copy(src, dst, in_sem.at[n]) for n, (src, dst) in enumerate(loads)]
-    for load in loads[:8]:
-        load.start()
+    def load(src, dst, n):
+        return pltpu.make_async_copy(src, dst, in_sem.at[n])
+
+    def landed(whole, sem):
+        pltpu.make_async_copy(whole, whole, sem).wait()
+
+    def load_streams():
+        for b in range(2):
+            rows = pl.ds(64 * b, 64)
+            for s in range(3):
+                load(g_hbm.at[0, s, rows], stage.at[b, s], b).start()
+            load(x_hbm.at[0, rows], stage.at[b, 3], b).start()
+
+    def load_rest():
+        load(gain_hbm, gain_v, 2).start()
+        load(w1_hbm.at[0], w1, 3).start()
+        for b in range(2):
+            for f in range(4):
+                load(r_hbm.at[0, pl.ds(64 * b, 64), pl.ds(256 * f, 256)], r_stage.at[b, f], 4).start()
+        load(w2_hbm.at[0], w2.at[pl.ds(0, 96)], 5).start()
 
     barrier = pltpu.get_barrier_semaphore()
 
     def greet(device):
         pl.semaphore_signal(barrier, inc=1, device_id=device, device_id_type=MESH)
 
-    for offset in ALL:
+    for offset in FAR:
         greet({"section": section(offset)})
-    for n in range(1, SHARDS):
+    greet({"tp": part ^ 5})
+    load_streams()
+    for offset in MIDDLE:
+        greet({"section": section(offset)})
+    for n in AROUND[1:]:
         greet({"tp": part ^ n})
-    for load in loads[8:]:
-        load.start()
+    for offset in CLOSE + NEXT:
+        greet({"section": section(offset)})
+    load_rest()
 
     class Exchange:
-        def __init__(self, peers, here, device, block, landing, ss, rs):
-            self.peers, self.here = peers, here
-
-            def copy(to, slot):
+        def __init__(self, peers, here, device, block, landing, bulk, n):
+            self.peers, self.here, self.bulk = peers, here, bulk
+            self.ss, self.rs = sems.at[2 * n], sems.at[2 * n + 1]
+
+            def copy(to):
                 return pltpu.make_async_remote_copy(
-                    src_ref=block(to), dst_ref=landing(slot), send_sem=ss.at[to], recv_sem=rs.at[slot],
+                    src_ref=block(to), dst_ref=landing(here), send_sem=self.ss, recv_sem=self.rs,
                     device_id=device(to), device_id_type=MESH,
                 )
 
@@ -108,15 +119,13 @@
 
         def send(self, peers=None):
             for to in peers or self.peers:
-                self.copy(to, self.here).start()
+                self.copy(to).start()
 
         def receive(self):
-            for to in self.peers:
-                self.copy(to, to).wait_recv()
+            landed(self.bulk, self.rs)
 
         def drain(self):
-            for to in self.peers:
-                self.copy(to, self.here).wait_send()
+            landed(self.bulk, self.ss)
 
     by_section = lambda to: {"section": to}
     by_part = lambda to: {"tp": to}
@@ -127,26 +136,25 @@
     parts = [part ^ n for n in AROUND]
     places = [place ^ n for n in range(1, PLACES)]
     planes = [(plane + n) & 7 for n in (4, 3, 5, 2, 6, 1, 7)]
-    xg = Exchange(sections, me, by_section, lambda p: sent.at[p], lambda p: held.at[p], x_ss, x_rs)
-    wx = Exchange(sections, me, by_section, lambda p: w_sent.at[p], lambda p: w_held.at[p], w_ss, w_rs)
-    ox = Exchange(sections, me, by_section, lambda p: o_sent.at[p], lambda p: o_held.at[p], o_ss, o_rs)
-    zx = Exchange(parts, part, by_part, lambda p: z_sent.at[p], lambda p: z_held.at[p], z_ss, z_rs)
-    ax = Exchange(parts, part, by_part, lambda p: act.at[part], lambda p: act.at[p], a_ss, a_rs)
-    dx = Exchange(parts, part, by_part, lambda p: d_sent.at[p], lambda p: d_held.at[p], d_ss, d_rs)
-    rx = Exchange(places, place, by_place, lambda p: r_sent.at[:, p], lambda p: r_held.at[p], r_ss, r_rs)
-    cx = Exchange(places, place, by_place, lambda p: c_sent.at[p], lambda p: c_held.at[:, p], c_ss, c_rs)
-    sx = Exchange(planes, plane, by_plane, lambda p: s_sent.at[p], lambda p: s_held.at[p], s_ss, s_rs)
+    xg = Exchange(sections, me, by_section, lambda p: sent.at[p], lambda p: held.at[p], held.at[pl.ds(0, 31)], 0)
+    wx = Exchange(sections, me, by_section, lambda p: w_sent.at[p], lambda p: w_held.at[p], w_held.at[pl.ds(0, 31)], 1)
+    ox = Exchange(sections, me, by_section, lambda p: o_sent.at[p], lambda p: o_held.at[p], o_held.at[pl.ds(0, 31)], 2)
+    zx = Exchange(parts, part, by_part, lambda p: z_sent.at[p], lambda p: z_held.at[p], z_held.at[pl.ds(0, 7)], 3)
+    ax = Exchange(parts, part, by_part, lambda p: act.at[part], lambda p: act.at[p], act.at[pl.ds(0, 7)], 4)
+    dx = Exchange(parts, part, by_part, lambda p: d_sent.at[p], lambda p: d_held.at[p], d_held.at[pl.ds(0, 7)], 5)
+    rx = Exchange(places, place, by_place, lambda p: r_sent.at[:, p], lambda p: r_held.at[p], r_held.at[pl.ds(0, 3)], 6)
+    cx = Exchange(places, place, by_place, lambda p: c_sent.at[p], lambda p: c_held.at[:, p], c_sent.at[pl.ds(0, 3)], 7)
+    sx = Exchange(planes, plane, by_plane, lambda p: s_sent.at[p], lambda p: s_held.at[p], s_held.at[pl.ds(0, 7)], 8)
 
     row, col = grid(256, 256)
     regroup = pick(((row >> 2) & 3) * 64 + (row >> 4) * 4 + (row & 3) == col)
 
     for b in range(2):
-        for load in loads[4 * b : 4 * b + 4]:
-            load.wait()
+        landed(stage.at[b], in_sem.at[b])
         grouped = dot(regroup, stage[b].reshape(256, WIDTH)).astype(BF16)
         sent[pl.ds(16 * b, 16)] = grouped.reshape(16, 16, WIDTH)
-    loads[8].wait()
-    loads[9].wait()
+    load(gain_hbm, gain_v, 2).wait()
+    load(w1_hbm.at[0], w1, 3).wait()
     gain = gain_v[...].astype(F32)
     x = jnp.concatenate([stage[0, 3], stage[1, 3]], axis=0).astype(F32)
     product = dot(jnp.concatenate(halves(x * gain), axis=0), w1[...])
@@ -156,11 +164,11 @@
     pl.semaphore_wait(barrier, SECTIONS - 1 + SHARDS - 1)
     zx.send()
     z_held[pl.ds(part, 1)] = z_sent[pl.ds(part, 1)]
-    xg.send(far + middle)
+    xg.send(middle + far)
     held[pl.ds(me, 1)] = sent[pl.ds(me, 1)]
 
-    for load in loads[10:]:
-        load.wait()
+    landed(r_stage, in_sem.at[4])
+    load(w2_hbm.at[0], w2.at[pl.ds(0, 96)], 5).wait()
     for b in range(2):
         grouped = dot(regroup, r_stage[b].reshape(256, 256)).astype(BF16)
         r_sent[pl.ds(4 * b, 4)] = grouped.reshape(4, PLACES, 16, 256)
@@ -267,25 +275,27 @@
 
     def e_copy(a, b):
         return pltpu.make_async_remote_copy(
-            src_ref=e_sent.at[a], dst_ref=e_held.at[me], send_sem=e_ss.at[a, b], recv_sem=e_rs.at[me],
+            src_ref=e_sent.at[a], dst_ref=e_held.at[me], send_sem=sems.at[18], recv_sem=sems.at[19],
             device_id={"section": SHARDS * a + part, "tp": b}, device_id_type=MESH,
         )
 
     def e_each(do):
-        for a in (2, 1, 3, 0):
+        for a in range(4):
             for n in AROUND:
-                do(e_copy((turn + a) & 3, part ^ n))
-        for a in range(4):
+                do(e_copy(a, part ^ n))
 
             @pl.when((home != part) | (turn != a))
-            def _():
+            def _(a=a):
                 do(e_copy(a, part))
 
-    def e_receive(n):
-        pltpu.make_async_remote_copy(
-            src_ref=e_sent.at[0], dst_ref=e_held.at[n], send_sem=e_ss.at[0, 0], recv_sem=e_rs.at[n],
-            device_id={"section": n, "tp": home}, device_id_type=MESH,
-        ).wait_recv()
+    def e_landed(sem):
+        @pl.when(home == part)
+        def _():
+            landed(e_held.at[pl.ds(0, 31)], sem)
+
+        @pl.when(home != part)
+        def _():
+            landed(e_held, sem)
 
     e_each(lambda copy: copy.start())
     ox.send(close + beside)
@@ -299,12 +309,7 @@
     for exchange in (zx, ax, rx, cx, sx, xg, wx, dx):
         exchange.drain()
 
-    for n in sections:
-        e_receive(n)
-
-    @pl.when(home != part)
-    def _():
-        e_receive(me)
+    e_landed(sems.at[19])
 
     mix_grad = e_held[...].reshape(TOKENS, 128)
     g_high, g_low = halves(mix_grad)
@@ -316,7 +321,7 @@
     inner = inverse * inverse * along / FULL_WIDTH
     local = inverse * (dot_nt(pre_grad, w1[...]) * gain)
 
-    e_each(lambda copy: copy.wait_send())
+    e_landed(sems.at[18])
     ox.drain()
     ox.receive()
     for b in range(2):
@@ -381,12 +386,7 @@
             by_part(16, 128), by_part(16, 128),
             pltpu.VMEM((4, 4, 128), F32),
             by_section(4, 128, F32),
-            dma((19,)),
-            *[dma((SECTIONS,)) for _ in range(6)],
-            *[dma((PLANES,)) for _ in range(2)],
-            *[dma((SHARDS,)) for _ in range(6)],
-            *[dma((PLACES,)) for _ in range(4)],
-            dma((4, SHARDS)), dma((SECTIONS,)),
+            dma((6,)), dma((20,)),
         ],
         compiler_params=pltpu.CompilerParams(
             collective_id=0, has_side_effects=True, vmem_limit_bytes=32 * 1024 * 1024

time: 56.2 us -> 52.7 us (0.938)
  Pallas kernels: 55.4 us -> 52 us
    pallas_call x1, Pallas kernels: 54.1 us -> 50.7 us  [local(): pl.pallas_call(kernel, out_shape=shapes, in_specs=[hbm] * 6, out_specs=(v...]
where the time goes in v4:
time: 52.7 us; the launch traced here: 52.6 us
  Pallas kernels  52 us (99%)
  between operations  0.64 us (1%)
    pallas_call x1, Pallas kernels, local(): pl.pallas_call(kernel, out_shape=shapes, in_specs=[hbm] * 6, out_specs=(v...  50.7 us
    pallas_call x1, Pallas kernels, local(): pl.pallas_call(handover, out_shape=shapes, in_specs=[vmem] * 3, out_specs...  1.29 us

profile of v4, /device:TPU:1, one launch (start us, length us, event | category | flops | bytes accessed | tf_op | source)
XLA Modules:
  0.0 52.6 jit_solution(9598955123512249984)
XLA Ops:
  0.6 50.7 %shard_map.85 = (bf16[1,128,1024]{2,1,0:T(8,128)(2,1)S(1)}, f32[1,1024,384]{2,1,0:T(8,128)S(1)}, f32[1,96,384]{2,1,0:T(8,128)S(1)}) custom-call(bf16[1,128,1024]{2,1,0:T(8,128)(2,1)} %x_hbm.1, bf16[1,3,128,1024]{3,2,1,0:T(8,128)(2,1)} %g_hbm.1, bf16[1,128,1024]{2,1,0:T(8,128)(2,1)} %r_hbm.1, bf16[1,1024]{1,0:T(2,128)(2,1)} %gain_hbm.1, ...), custom_call_target="tpu_custom_call" | custom-call | tf_op jit(solution)/shard_map/pallas_call | solution.py:359
  51.3 1.3 %shard_map.86 = (bf16[1,128,1024]{2,1,0:T(8,128)(2,1)}, f32[1,1024,384]{2,1,0:T(8,128)}, f32[1,96,384]{2,1,0:T(8,128)}) custom-call(bf16[1,128,1024]{2,1,0:T(8,128)(2,1)S(1)} %get-tuple-element.9.out_in, f32[1,1024,384]{2,1,0:T(8,128)S(1)} %get-tuple-element.10.first_in, f32[1,96,384]{2,1,0:T(8,128)S(1)} %get-tuple-element.11.second_in), custom_call_target="tpu_custom_call" | custom-call | tf_op jit(solution)/shard_map/pallas_call | solution.py:395

commit v5 on v4

--- a/solution.py
+++ b/solution.py
@@ -11,6 +11,7 @@
 F32, BF16 = jnp.float32, jnp.bfloat16
 SECTIONS, SHARDS = 32, 8
 PLANES, PLACES = 8, 4
+PIECES = 4
 TOKENS, WIDTH, HIDDEN = 128, 1024, 384
 FULL_WIDTH = WIDTH * SHARDS
 C0, C1 = 0.7978845608028654, 0.044715
@@ -52,8 +53,8 @@
 
 def kernel(
     x_hbm, g_hbm, r_hbm, gain_hbm, w1_hbm, w2_hbm,
-    out_v, first_v, second_v,
-    stage, r_stage, gain_v, w1, w2, spread_m, sel_m, fold_m, across_m, wide_m, same_m, kept_m, ungroup_m, normed_t,
+    out_v, normed_t, pre_v, second_v,
+    stage, r_stage, gain_v, w1, w2, spread_m, sel_m, fold_m, across_m, wide_m, same_m, kept_m, ungroup_m,
     sent, held, r_sent, r_held, c_sent, c_held, s_sent, s_held, w_sent, w_held, o_sent, o_held,
     z_sent, z_held, act, d_sent, d_held, e_sent, e_held,
     in_sem, sems,
@@ -314,7 +315,7 @@
     mix_grad = e_held[...].reshape(TOKENS, 128)
     g_high, g_low = halves(mix_grad)
     pre_grad = ((dot(g_high, w2[...]) + dot(g_low, w2[...])) * slope).astype(BF16)
-    first_v[0] = dot(normed_t[...], pre_grad)
+    pre_v[...] = pre_grad
     second = dot_tn(g_high, h_high) + dot_tn(g_low, h_high) + dot_tn(g_high, h_low)
     second_v[0] = second[:96]
     along = jnp.sum(pre_grad.astype(F32) * pre, axis=1, keepdims=True)
@@ -334,11 +335,19 @@
             out_v[0, pl.ds(64 * b, 64), pl.ds(256 * f, 256)] = value.astype(BF16)
 
 
-def handover(out_in, first_in, second_in, out, first, second, sems):
-    pairs = ((first_in, first), (out_in, out), (second_in, second))
-    copies = [pltpu.make_async_copy(src, dst, sems.at[n]) for n, (src, dst) in enumerate(pairs)]
+def handover(out_in, normed_t, pre_grad, second_in, out, first, second, first_v, sems):
+    copies = [
+        pltpu.make_async_copy(out_in, out, sems.at[0]),
+        pltpu.make_async_copy(second_in, second, sems.at[1]),
+    ]
     for copy in copies:
         copy.start()
+    step = WIDTH // PIECES
+    for n in range(PIECES):
+        rows = pl.ds(step * n, step)
+        first_v[rows] = dot(normed_t[rows], pre_grad[...])
+        copies.append(pltpu.make_async_copy(first_v.at[rows], first.at[0, rows], sems.at[2 + n]))
+        copies[-1].start()
     for copy in copies:
         copy.wait()
 
@@ -358,9 +367,14 @@
     args = (layer_outputs, stream_grads, residual_grads, norm_gain, first_weight, jnp.swapaxes(second_weight, 1, 2))
     grads = pl.pallas_call(
         kernel,
-        out_shape=shapes,
+        out_shape=(
+            shapes[0],
+            jax.ShapeDtypeStruct((WIDTH, TOKENS), BF16),
+            jax.ShapeDtypeStruct((TOKENS, HIDDEN), BF16),
+            shapes[2],
+        ),
         in_specs=[hbm] * 6,
-        out_specs=(vmem, vmem, vmem),
+        out_specs=(vmem,) * 4,
         scratch_shapes=[
             pltpu.VMEM((2, 4, 64, WIDTH), BF16),
             pltpu.VMEM((2, 4, 64, 256), BF16),
@@ -375,7 +389,6 @@
             pltpu.VMEM((512, 128), F32),
             pltpu.VMEM((512, 128), F32),
             pltpu.VMEM((256, 256), BF16),
-            pltpu.VMEM((WIDTH, TOKENS), BF16),
             by_section(16, WIDTH, BF16), by_section(16, WIDTH, BF16),
             by_place(PLANES, PLACES), by_place(PLACES, PLANES),
             by_place(PLACES, PLANES), by_place(PLANES, PLACES),
@@ -395,9 +408,9 @@
     grads = pl.pallas_call(
         handover,
         out_shape=shapes,
-        in_specs=[vmem] * 3,
+        in_specs=[vmem] * 4,
         out_specs=(hbm,) * 3,
-        scratch_shapes=[dma((3,))],
+        scratch_shapes=[pltpu.VMEM((WIDTH, HIDDEN), F32), dma((PIECES + 2,))],
         compiler_params=pltpu.CompilerParams(vmem_limit_bytes=8 * 1024 * 1024),
     )(*[pltpu.with_memory_space_constraint(g, pltpu.VMEM) for g in grads])
     return grads[0], grads[1], jnp.swapaxes(grads[2], 1, 2)

time: 52.7 us -> 52.9 us (level)
  no operation moved by 1% of the time
where the time goes in v5:
time: 52.9 us; the launch traced here: 52.8 us
  Pallas kernels  52.1 us (98%)
  between operations  0.64 us (1%)
    pallas_call x1, Pallas kernels, local(): pl.pallas_call(kernel, out_shape=(shapes[0], jax.ShapeDtypeStruct((WIDTH,...  50.7 us
    pallas_call x1, Pallas kernels, local(): pl.pallas_call(handover, out_shape=shapes, in_specs=[vmem] * 4, out_specs...  1.4 us

profile of v5, /device:TPU:1, one launch (start us, length us, event | category | flops | bytes accessed | tf_op | source)
XLA Modules:
  0.0 52.8 jit_solution(402378117946071379)
XLA Ops:
  0.6 50.7 %shard_map.85 = (bf16[1,128,1024]{2,1,0:T(8,128)(2,1)S(1)}, bf16[1024,128]{1,0:T(8,128)(2,1)S(1)}, bf16[128,384]{1,0:T(8,128)(2,1)S(1)}, f32[1,96,384]{2,1,0:T(8,128)S(1)}) custom-call(bf16[1,128,1024]{2,1,0:T(8,128)(2,1)} %x_hbm.1, bf16[1,3,128,1024]{3,2,1,0:T(8,128)(2,1)} %g_hbm.1, bf16[1,128,1024]{2,1,0:T(8,128)(2,1)} %r_hbm.1, bf16[1,1024]{1,0:T(2,128)(2,1)} %gain_hbm.1, ...), custom_call_target="tpu_custom_call" | custom-call | tf_op jit(solution)/shard_map/pallas_call | solution.py:368
  51.4 1.4 %shard_map.86 = (bf16[1,128,1024]{2,1,0:T(8,128)(2,1)}, f32[1,1024,384]{2,1,0:T(8,128)}, f32[1,96,384]{2,1,0:T(8,128)}) custom-call(bf16[1,128,1024]{2,1,0:T(8,128)(2,1)S(1)} %get-tuple-element.10.out_in, bf16[1024,128]{1,0:T(8,128)(2,1)S(1)} %get-tuple-element.11.normed_t, bf16[128,384]{1,0:T(8,128)(2,1)S(1)} %get-tuple-element.12.pre_grad, ...), custom_call_target="tpu_custom_call" | custom-call | tf_op jit(solution)/shard_map/pallas_call | solution.py:408

commit v6 on v4

--- a/solution.py
+++ b/solution.py
@@ -263,7 +263,7 @@
         o_sent[pl.ds(16 * b, 16)] = block.astype(BF16).reshape(16, 16, 256)
     o_held[pl.ds(me, 1)] = o_sent[pl.ds(me, 1)]
 
-    ox.send(far + middle)
+    ox.send(middle + far)
     dx.receive()
     total = d_held[0]
     for p in range(1, SHARDS):
@@ -298,7 +298,7 @@
             landed(e_held, sem)
 
     e_each(lambda copy: copy.start())
-    ox.send(close + beside)
+    ox.send(beside + close)
 
     @pl.when(home == part)
     def _():

time: 52.7 us -> 52.5 us (level)
  Pallas kernels: 52 us -> 51.2 us
    pallas_call x1, Pallas kernels: 50.7 us -> 50 us  [local(): pl.pallas_call(kernel, out_shape=shapes, in_specs=[hbm] * 6, out_specs=(v...]
where the time goes in v6:
time: 52.5 us; the launch traced here: 51.9 us
  Pallas kernels  51.2 us (98%)
  between operations  0.64 us (1%)
    pallas_call x1, Pallas kernels, local(): pl.pallas_call(kernel, out_shape=shapes, in_specs=[hbm] * 6, out_specs=(v...  50 us
    pallas_call x1, Pallas kernels, local(): pl.pallas_call(handover, out_shape=shapes, in_specs=[vmem] * 3, out_specs...  1.29 us

profile of v6, /device:TPU:1, one launch (start us, length us, event | category | flops | bytes accessed | tf_op | source)
XLA Modules:
  0.0 51.9 jit_solution(7033122323809422493)
XLA Ops:
  0.6 50.0 %shard_map.85 = (bf16[1,128,1024]{2,1,0:T(8,128)(2,1)S(1)}, f32[1,1024,384]{2,1,0:T(8,128)S(1)}, f32[1,96,384]{2,1,0:T(8,128)S(1)}) custom-call(bf16[1,128,1024]{2,1,0:T(8,128)(2,1)} %x_hbm.1, bf16[1,3,128,1024]{3,2,1,0:T(8,128)(2,1)} %g_hbm.1, bf16[1,128,1024]{2,1,0:T(8,128)(2,1)} %r_hbm.1, bf16[1,1024]{1,0:T(2,128)(2,1)} %gain_hbm.1, ...), custom_call_target="tpu_custom_call" | custom-call | tf_op jit(solution)/shard_map/pallas_call | solution.py:359
  50.6 1.3 %shard_map.86 = (bf16[1,128,1024]{2,1,0:T(8,128)(2,1)}, f32[1,1024,384]{2,1,0:T(8,128)}, f32[1,96,384]{2,1,0:T(8,128)}) custom-call(bf16[1,128,1024]{2,1,0:T(8,128)(2,1)S(1)} %get-tuple-element.9.out_in, f32[1,1024,384]{2,1,0:T(8,128)S(1)} %get-tuple-element.10.first_in, f32[1,96,384]{2,1,0:T(8,128)S(1)} %get-tuple-element.11.second_in), custom_call_target="tpu_custom_call" | custom-call | tf_op jit(solution)/shard_map/pallas_call | solution.py:395
